TPU v7x, 256 devices: a whole 4x4x8 slice. The times are simulated.
256 devices in a mesh: dp: 8 (over x_hi, y), ctx: 32 (over z, x_lo, core).
Axes of the slice: x: 4 (x_hi: 2, x_lo: 2; x = x_hi * 2 + x_lo), y: 4, z: 8, core: 2. Of those that a mesh axis runs over, the one named last changes fastest.
Arguments:
- q_nope: bfloat16 [8, 4096, 8192], P('dp', 'ctx'), may hold values from -6 to 6
- q_rope: bfloat16 [8, 4096, 4096], P('dp', 'ctx'), may hold values from -6 to 6
- grad_out: bfloat16 [8, 4096, 8192], P('dp', 'ctx'), may hold values from -6 to 6
- log_total: float32 [8, 64, 4096], P('dp', None, 'ctx'), may hold values from 5 to 6.5
- kv_latent: bfloat16 [8, 4096, 320], P('dp', 'ctx'), may hold values from -6 to 6
- up_weight: bfloat16 [256, 16384], P('ctx'), may hold values from -0.375 to 0.375
- selected: int32 [8, 64, 3], P('dp', 'ctx'), may hold values from -1 to 62, as said below
- offered: int32 [8, 32, 4], P('dp'), may hold values from 0 to 1, as said below
Outputs:
- grad_q_nope: bfloat16 [8, 4096, 8192], P('dp', 'ctx')
- grad_q_rope: bfloat16 [8, 4096, 4096], P('dp', 'ctx')
- grad_latent: float32 [8, 4096, 320], P('dp', 'ctx')
- grad_weight: float32 [256, 16384], P('ctx')
Inputs may be any that keep to these rules, and one draw needn't show every extreme that they name: offered[b, s, m] is a block number within group s's 128/64 blocks; in matching m group s offers it to group s + m + 1. `selected`: each list holds distinct global block ids, then -1 entries; every id is an earlier block of the query block's own group or a block offered to that group in one of the four matchings; a query block that is not the first of its group always lists the block just before it.
All inputs are finite; a program needn't handle non-finite values.
Results may differ from a plain program's by a relative error of at most 0.0028.
The roundings to bfloat16 on the way count: a program that leaves them out, or rounds other values in their place, can miss the bound.
Values may be sent and summed in bfloat16 or wider, within the bound.
A program may use at most 192 MiB of HBM per device.

v0:
```python
import jax
import jax.numpy as jnp
from jax import lax
from jax.sharding import PartitionSpec as P

LAT = 256
ROPE = 64
NOPE = 128
VDIM = 128
BLOCK = 64


partner_offsets = (1, 2, 3, 4)


def from_behind(value, axis, steps):
    count = lax.axis_size(axis)
    initial, last = (max(0, -steps), min(count, count - steps))
    return lax.ppermute(value, axis, [(source, source + steps) for source in range(initial, last)])


def allowed_mask(selection, key_ids, first_query):
    query_ids = first_query + jnp.arange(selection.shape[0], dtype=jnp.int32)
    same_block = key_ids[None, :] == query_ids[:, None]
    picked = (
        jnp.any(selection[:, :, None] == key_ids[None, None, :], axis=1) & (key_ids >= 0)[None, :]
    )
    inner = jnp.arange(BLOCK, dtype=jnp.int32)
    causal = inner[:, None] >= inner[None, :]
    block_mask = picked[:, None, :, None] | same_block[:, None, :, None] & causal[None, :, None, :]
    return block_mask.reshape(selection.shape[0] * BLOCK, key_ids.shape[0] * BLOCK)


def head_backward(
    queries, rope_queries, out_grads, totals, key_part, value_part, rope_keys, allowed
):
    softmax_scale = 1.0 / jnp.sqrt(jnp.float32(NOPE + ROPE))
    scores = (
        jnp.einsum("qhd,khd->hqk", queries, key_part, preferred_element_type=jnp.float32)
        + jnp.einsum("qhd,kd->hqk", rope_queries, rope_keys, preferred_element_type=jnp.float32)
    ) * softmax_scale
    probabilities = jnp.where(allowed[None], jnp.exp(scores - totals[:, :, None]), jnp.float32(0.0))
    prob_grads = jnp.einsum(
        "qhd,khd->hqk", out_grads, value_part, preferred_element_type=jnp.float32
    )
    row_dot = jnp.sum(probabilities * prob_grads, axis=2, keepdims=True)
    score_grads = (probabilities * (prob_grads - row_dot)).astype(jnp.bfloat16)
    probs_low = probabilities.astype(jnp.bfloat16)
    grad_nope = (
        jnp.einsum("hqk,khd->qhd", score_grads, key_part, preferred_element_type=jnp.float32)
        * softmax_scale
    ).astype(jnp.bfloat16)
    grad_rope = (
        jnp.einsum("hqk,kd->qhd", score_grads, rope_keys, preferred_element_type=jnp.float32)
        * softmax_scale
    ).astype(jnp.bfloat16)
    key_grad = (
        jnp.einsum("hqk,qhd->khd", score_grads, queries, preferred_element_type=jnp.float32)
        * softmax_scale
    )
    value_grad = jnp.einsum(
        "hqk,qhd->khd", probs_low, out_grads, preferred_element_type=jnp.float32
    )
    both_grads = jnp.concatenate([key_grad, value_grad], axis=2).astype(jnp.bfloat16)
    rope_grad = (
        jnp.einsum("hqk,qhd->kd", score_grads, rope_queries, preferred_element_type=jnp.float32)
        * softmax_scale
    )
    return (grad_nope, grad_rope, both_grads, rope_grad)


def group_backward(queries, rope_queries, out_grads, totals, candidates, weight, allowed):
    latent_cols = candidates[:, :LAT]
    rope_keys = candidates[:, LAT:]
    expanded = jnp.dot(latent_cols, weight, preferred_element_type=jnp.float32).astype(jnp.bfloat16)
    query_len = queries.shape[0]
    key_len = candidates.shape[0]
    head_count = totals.shape[0]
    per_group = 8
    groups = head_count // per_group

    def regroup(array, width, length):
        return array.reshape(length, groups, per_group, width).transpose(1, 0, 2, 3)

    both_parts = regroup(expanded, NOPE + VDIM, key_len)
    items = (
        regroup(queries, NOPE, query_len),
        regroup(rope_queries, ROPE, query_len),
        regroup(out_grads, VDIM, query_len),
        totals.reshape(groups, per_group, query_len),
        both_parts[..., :NOPE],
        both_parts[..., NOPE:],
    )

    def one_heads(entry):
        return head_backward(
            entry[0], entry[1], entry[2], entry[3], entry[4], entry[5], rope_keys, allowed
        )

    results = lax.map(one_heads, items)
    grad_nope = results[0].transpose(1, 0, 2, 3).reshape(query_len, head_count * NOPE)
    grad_rope = results[1].transpose(1, 0, 2, 3).reshape(query_len, head_count * ROPE)
    key_grads = results[2].transpose(1, 0, 2, 3).reshape(key_len, head_count * (NOPE + VDIM))
    rope_part = jnp.sum(results[3], axis=0)
    latent_grad = lax.dot_general(
        key_grads, weight, (((1,), (1,)), ((), ())), preferred_element_type=jnp.float32
    )
    cand_grad = jnp.concatenate([latent_grad, rope_part], axis=1)
    return (grad_nope, grad_rope, key_grads, cand_grad)


def shards(q_nope, q_rope, grad_out, log_total, kv_latent, up_weight, selected, offered):
    group_index = lax.axis_index("ctx")
    group_len = kv_latent.shape[1]
    per_block = group_len // BLOCK
    weight = lax.all_gather(up_weight, "ctx", axis=0, tiled=True)
    own_rows = kv_latent[0]
    offer_plan = offered[0]
    pieces = [own_rows]
    piece_ids = [group_index * per_block + jnp.arange(per_block, dtype=jnp.int32)]
    for matching, offset in enumerate(partner_offsets):
        block_index = offer_plan[group_index, matching]
        block_rows = lax.dynamic_slice_in_dim(own_rows, block_index * BLOCK, BLOCK, 0)
        pieces.append(from_behind(block_rows, "ctx", offset))
        source = group_index - offset
        sender = jnp.maximum(source, 0)
        piece_ids.append(
            jnp.where(source >= 0, sender * per_block + offer_plan[sender, matching], -1)[None]
        )
    candidates = jnp.concatenate(pieces, axis=0)
    key_ids = jnp.concatenate(piece_ids, axis=0)
    allowed = allowed_mask(selected[0], key_ids, group_index * per_block)
    grad_nope, grad_rope, key_grads, cand_grad = group_backward(
        q_nope[0], q_rope[0], grad_out[0], log_total[0], candidates, weight, allowed
    )
    grad_rows = cand_grad[:group_len]
    for matching, offset in enumerate(partner_offsets):
        outgoing = cand_grad[group_len + matching * BLOCK : group_len + (matching + 1) * BLOCK]
        returned = from_behind(outgoing, "ctx", -offset)
        first_row = offer_plan[group_index, matching] * BLOCK
        current = lax.dynamic_slice_in_dim(grad_rows, first_row, BLOCK, 0)
        grad_rows = lax.dynamic_update_slice_in_dim(grad_rows, current + returned, first_row, 0)
    latent_cols = candidates[:, :LAT]
    shard_sum = lax.psum_scatter(
        lax.dot_general(
            latent_cols, key_grads, (((0,), (0,)), ((), ())), preferred_element_type=jnp.float32
        ),
        "ctx",
        scatter_dimension=0,
        tiled=True,
    )
    grad_weight = lax.psum(shard_sum, "dp")
    return (grad_nope[None], grad_rope[None], grad_rows[None], grad_weight)


def solution(mesh):
    in_specs = (
        P("dp", "ctx", None),
        P("dp", "ctx", None),
        P("dp", "ctx", None),
        P("dp", None, "ctx"),
        P("dp", "ctx", None),
        P("ctx", None),
        P("dp", "ctx", None),
        P("dp", None, None),
    )
    out_specs = (P("dp", "ctx", None), P("dp", "ctx", None), P("dp", "ctx", None), P("ctx", None))
    return jax.shard_map(shards, mesh=mesh, in_specs=in_specs, out_specs=out_specs, check_vma=False)
```

profile of v0, /device:TPU:1, one launch (start us, length us, event | category | flops | bytes accessed | tf_op | source)
XLA Modules:
  0.0 551.9 jit_solution(4230466064307262618)
XLA Ops:
  14.0 4.4 collective-permute-start.3
  18.3 3.1 collective-permute-start.1
  21.5 4.6 collective-permute-start
  26.1 2.6 collective-permute-start.2
  34.6 3.2 copy.34
  37.8 4.1 copy.36
  43.0 44.4 %all-gather.2.cloned.1.call-done = bf16[256,16384]{1,0:T(8,128)(2,1)} async-done(((bf16[8,16384]{1,0:T(8,128)(2,1)}), bf16[256,16384]{1,0:T(8,128)(2,1)}) %all-gather.2.cloned.1.call-update) | async-done | bytes 8388624 | tf_op jit(solution)/shard_map/all_gather | solution.py:116
  87.4 11.4 %convolution_convert_fusion.1 = bf16[384,16384]{1,0:T(8,128)(2,1)} fusion(bf16[256,16384]{1,0:T(8,128)(2,1)} %all-gather.2.cloned.1.call-done, bf16[384,320]{0,1:T(8,128)(2,1)S(1)} %concatenate.28), kind=kOutput, calls=%fused_computation.57 | convolution fusion | flops 3227516928 | bytes 21168128 | tf_op jit(solution)/shard_map/dot_general | solution.py:75
  98.8 7.9 %copy.47 = bf16[48,8,64,256]{3,2,1,0:T(8,128)(2,1)S(1)} copy(bf16[48,8,64,256]{3,1,2,0:T(8,128)(2,1)} %bitcast.184) | data formatting | bytes 25165824
  106.7 20.5 %copy.49 = bf16[384,8,8,256]{3,0,2,1:T(8,128)(2,1)S(1)} copy(bf16[384,8,8,256]{3,2,1,0:T(8,128)(2,1)S(1)} %bitcast.183) | data formatting | bytes 25165824 | tf_op jit(solution)/shard_map/reshape | solution.py:83
  127.3 5.8 %fusion.54 = (bf16[8,384,8,128]{3,1,2,0:T(8,128)(2,1)}, bf16[8,384,8,128]{3,1,2,0:T(8,128)(2,1)}) fusion(bf16[8,384,8,256]{3,1,2,0:T(8,128)(2,1)S(1)} %bitcast.182), kind=kLoop, calls=%fused_computation.97 | loop fusion | bytes 25165824 | tf_op jit(solution)/shard_map/slice | solution.py:92
  133.0 111.6 %while.17 = (s32[]{:T(128)}, bf16[8,128,8,128]{1,3,2,0:T(8,128)(2,1)}, bf16[8,128,8,64]{1,3,2,0:T(8,128)(2,1)}, bf16[8,384,8,256]{1,3,2,0:T(8,128)(2,1)}, f32[8,...) while((s32[]{:T(128)}, ...), condition=%wide.region_3.4_spmd.clone, body=%wide.region_1.3_spmd.clone.sunk | while | flops 663084032 | bytes 25718988 | solution.py:100
  157.3 2.3 fusion.101
  185.2 2.3 fusion.101
  199.1 2.3 fusion.101
  213.1 2.3 fusion.101
  227.1 2.3 fusion.101
  241.0 2.3 fusion.101
  244.6 15.8 %fusion.47 = f32[256,16384]{1,0:T(8,128)} fusion(bf16[384,16384]{0,1:T(8,128)(2,1)} %bitcast.185, bf16[384,320]{0,1:T(8,128)(2,1)S(1)} %copy-done.1), kind=kOutput, calls=%fused_computation.67 | convolution fusion | flops 3221225472 | bytes 29556736 | tf_op jit(solution)/shard_map/dot_general | solution.py:145
  262.0 2.9 copy.44
  265.0 10.9 %fusion.55 = f32[384,256]{0,1:T(8,128)S(1)} fusion(bf16[256,16384]{1,0:T(8,128)(2,1)} %all-gather.2.cloned.1.call-done, bf16[384,16384]{0,1:T(8,128)(2,1)} %bitcast.186), kind=kOutput, calls=%fused_computation.98 | convolution fusion | flops 3221225472 | bytes 21364736 | tf_op jit(solution)/shard_map/dot_general | solution.py:105
  283.3 6.6 %collective-permute-done.4 = f32[64,320]{0,1:T(8,128)S(1)} collective-permute-done((f32[64,320]{0,1:T(8,128)S(1)}, f32[64,320]{0,1:T(8,128)S(1)}, u32[]{:S(2)}, u32[]{:S(2)}) %collective-permute-start.4) | collective-permute-done | bytes 81952 | tf_op jit(solution)/shard_map/ppermute | solution.py:19
  291.1 163.8 %reduce-scatter.2.cloned.1.call-done = f32[8,16384]{1,0:T(8,128)} async-done(((f32[256,16384]{1,0:T(8,128)}), f32[8,16384]{1,0:T(8,128)}) %reduce-scatter.2.cloned.1.call-update) | async-done | bytes 524304 | tf_op jit(solution)/shard_map/reduce_scatter | solution.py:144
  458.2 85.3 %all-reduce.2.cloned.1.call-done = f32[8,16384]{1,0:T(8,128)} async-done(((f32[8,16384]{1,0:T(8,128)}), f32[8,16384]{1,0:T(8,128)}) %all-reduce.2.cloned.1.call-update) | async-done | bytes 524304 | tf_op jit(solution)/shard_map/psum | solution.py:152
  (156 shorter events, 121.0 us)
Async XLA Ops:
  7.2 80.3 %all-gather.2.cloned.1.call-start = ((), (), s32[]{:S(2)}) async-start(), calls=%async_computation.1 | async-start | bytes 8650752 | tf_op jit(solution)/shard_map/all_gather | solution.py:116
  7.9 447.0 %reduce-scatter.2.cloned.1.call-start = ((), (), s32[]{:S(2)}) async-start(), calls=%async_computation.2 | async-start | bytes 17301504 | tf_op jit(solution)/shard_map/reduce_scatter | solution.py:144
  14.0 28.0 %collective-permute-start.3 = (bf16[64,320]{0,1:T(8,128)(2,1)}, bf16[64,320]{0,1:T(8,128)(2,1)S(1)}, u32[]{:S(2)}, u32[]{:S(2)}) collective-permute-start(bf16[64,320]{0,1:T(8,128)(2,1)} %get-tuple-element.189), channel_id=1, source_target_pairs={{0,4},{1,5},{2,6},{3,7},{4,8},{5,9},{6,10},{7,11},{8,12},{9,13},{1... | collective-permute-start | bytes 122888 | tf_op jit(solution)/shard_map/ppermute | solution.py:19
  18.3 23.6 %collective-permute-start.1 = (bf16[64,320]{0,1:T(8,128)(2,1)S(1)}, bf16[64,320]{0,1:T(8,128)(2,1)S(1)}, u32[]{:S(2)}, u32[]{:S(2)}) collective-permute-start(bf16[64,320]{0,1:T(8,128)(2,1)S(1)} %get-tuple-element.190), channel_id=1, source_target_pairs={{0,2},{1,3},{2,4},{3,5},{4,6},{5,7},{6,8},{7,9},{8,10},{9,11},{10,... | collective-permute-start | bytes 122888 | tf_op jit(solution)/shard_map/ppermute | solution.py:19
  21.5 20.5 %collective-permute-start = (bf16[64,320]{0,1:T(8,128)(2,1)S(1)}, bf16[64,320]{0,1:T(8,128)(2,1)S(1)}, u32[]{:S(2)}, u32[]{:S(2)}) collective-permute-start(bf16[64,320]{0,1:T(8,128)(2,1)S(1)} %get-tuple-element.191), channel_id=1, source_target_pairs={{0,1},{1,2},{2,3},{3,4},{4,5},{5,6},{6,7},{7,8},{8,9},{9,10},{10,1... | collective-permute-start | bytes 122888 | tf_op jit(solution)/shard_map/ppermute | solution.py:19
  26.1 15.8 %collective-permute-start.2 = (bf16[64,320]{0,1:T(8,128)(2,1)S(1)}, bf16[64,320]{0,1:T(8,128)(2,1)}, u32[]{:S(2)}, u32[]{:S(2)}) collective-permute-start(bf16[64,320]{0,1:T(8,128)(2,1)S(1)} %get-tuple-element.192), channel_id=1, source_target_pairs={{0,3},{1,4},{2,5},{3,6},{4,7},{5,8},{6,9},{7,10},{8,11},{9,12},{10... | collective-permute-start | bytes 122888 | tf_op jit(solution)/shard_map/ppermute | solution.py:19
  37.8 4.2 copy-start.4
  43.0 55.8 %copy-start = (bf16[384,320]{0,1:T(8,128)(2,1)}, bf16[384,320]{0,1:T(8,128)(2,1)S(1)}, u32[]{:S(2)}) copy-start(bf16[384,320]{0,1:T(8,128)(2,1)S(1)} %concatenate.28) | copy-start | bytes 737284
  127.2 5.8 %slice-start = ((bf16[384,320]{0,1:T(8,128)(2,1)}), bf16[384,64]{0,1:T(8,128)(2,1)S(1)}, s32[]{:S(2)}) async-start(bf16[384,320]{0,1:T(8,128)(2,1)} %copy-done), calls=%async_computation.4 | async-start | bytes 98304 | tf_op jit(solution)/shard_map/slice | solution.py:74
  133.0 111.6 %copy-start.1 = (bf16[384,320]{0,1:T(8,128)(2,1)S(1)}, bf16[384,320]{0,1:T(8,128)(2,1)}, u32[]{:S(2)}) copy-start(bf16[384,320]{0,1:T(8,128)(2,1)} %copy-done) | copy-start | bytes 737284
  260.4 1.6 copy-start.3
  260.5 283.0 %all-reduce.2.cloned.1.call-start = ((), (), s32[]{:S(2)}) async-start(), calls=%async_computation.3 | async-start | bytes 1048576 | tf_op jit(solution)/shard_map/psum | solution.py:152
  265.0 17.0 %copy-start.5 = (bf16[8,128,8,64]{1,3,2,0:T(8,128)(2,1)S(1)}, bf16[8,128,8,64]{1,3,2,0:T(8,128)(2,1)}, u32[]{:S(2)}) copy-start(bf16[8,128,8,64]{1,3,2,0:T(8,128)(2,1)} %get-tuple-element.75) | copy-start | bytes 3145732
  276.1 180.9 %collective-permute-start.7 = (f32[64,320]{0,1:T(8,128)S(1)}, f32[64,320]{0,1:T(8,128)S(1)}, u32[]{:S(2)}, u32[]{:S(2)}) collective-permute-start(f32[64,320]{0,1:T(8,128)S(1)} %get-tuple-element.185), channel_id=1, source_target_pairs={{4,0},{5,1},{6,2},{7,3},{8,4},{9,5},{10,6},{11,7},{12,8},{13,9},{1... | collective-permute-start | bytes 245768 | tf_op jit(solution)/shard_map/ppermute | solution.py:19
  277.4 12.5 %collective-permute-start.4 = (f32[64,320]{0,1:T(8,128)S(1)}, f32[64,320]{0,1:T(8,128)S(1)}, u32[]{:S(2)}, u32[]{:S(2)}) collective-permute-start(f32[64,320]{0,1:T(8,128)S(1)} %get-tuple-element.186), channel_id=1, source_target_pairs={{1,0},{2,1},{3,2},{4,3},{5,4},{6,5},{7,6},{8,7},{9,8},{10,9},{11,1... | collective-permute-start | bytes 245768 | tf_op jit(solution)/shard_map/ppermute | solution.py:19
  279.3 175.6 %collective-permute-start.5 = (f32[64,320]{0,1:T(8,128)S(1)}, f32[64,320]{0,1:T(8,128)S(1)}, u32[]{:S(2)}, u32[]{:S(2)}) collective-permute-start(f32[64,320]{0,1:T(8,128)S(1)} %get-tuple-element.187), channel_id=1, source_target_pairs={{2,0},{3,1},{4,2},{5,3},{6,4},{7,5},{8,6},{9,7},{10,8},{11,9},{12,... | collective-permute-start | bytes 245768 | tf_op jit(solution)/shard_map/ppermute | solution.py:19
  280.6 175.2 %collective-permute-start.6 = (f32[64,320]{0,1:T(8,128)S(1)}, f32[64,320]{0,1:T(8,128)S(1)}, u32[]{:S(2)}, u32[]{:S(2)}) collective-permute-start(f32[64,320]{0,1:T(8,128)S(1)} %get-tuple-element.188), channel_id=1, source_target_pairs={{3,0},{4,1},{5,2},{6,3},{7,4},{8,5},{9,6},{10,7},{11,8},{12,9},{13... | collective-permute-start | bytes 245768 | tf_op jit(solution)/shard_map/ppermute | solution.py:19
  458.2 87.2 %copy-start.2 = (f32[1,128,320]{1,2,0:T(8,128)}, f32[1,128,320]{1,2,0:T(8,128)S(1)}, u32[]{:S(2)}) copy-start(f32[1,128,320]{1,2,0:T(8,128)S(1)} %dynamic_update_slice.32) | copy-start | bytes 491524
Sparse Core Ops, SparseCore 0:
  9.9 77.5 all-gather.1
  260.6 194.2 reduce-scatter.1
  457.6 85.8 all-reduce.1
where the time goes:
time: 559 us; the launch traced here: 552 us
  waiting for transfers between devices  301 us (54%)
  matrix products  128 us (23%)
  local copies, waits for them, and re-layouts  67.3 us (12%)
  starting transfers between devices  20.6 us (4%)
  between operations  19.1 us (3%)
  other arithmetic  15.1 us (3%)
    reduce_scatter x1, waiting for transfers between devices, shards(): lax.psum_scatter(lax.dot_general(latent_cols, key_grads, (((0,), (0,)), (...  164 us
    psum x1, waiting for transfers between devices, shards(): grad_weight = lax.psum(shard_sum, 'dp')  85.3 us
    all_gather x1, waiting for transfers between devices, shards(): weight = lax.all_gather(up_weight, 'ctx', axis=0, tiled=True)  44.4 us
    unnamed x18, local copies, waits for them, and re-layouts  22.3 us
    ppermute x8, starting transfers between devices, from_behind(): lax.ppermute(value, axis, [(source, source + steps) for source in range(i...  20.5 us
    reshape x1, local copies, waits for them, and re-layouts, regroup(): return array.reshape(length, groups, per_group, width).transpose(1, 0, 2, 3)  20.5 us
    dot_general x8, matrix products, head_backward(): jnp.einsum('hqk,khd->qhd', score_grads, key_part, preferred_element_type=...  18.6 us
    dot_general x1, matrix products, shards(): lax.dot_general(latent_cols, key_grads, (((0,), (0,)), ((), ())), preferr...  15.8 us
  transfers between devices with their start and end apart: 11, of which 4 were waited for; matrix products, arithmetic and copies ran while one was open for 6% of the time, Pallas kernels for 0%

commit v1 on v0

v1 whole, which is shorter than its diff:
```python
import functools

import jax
import jax.numpy as jnp
from jax import lax
from jax.experimental import pallas as pl
from jax.experimental.pallas import tpu as pltpu
from jax.sharding import PartitionSpec as P

LAT = 256
ROPE = 64
NOPE = 128
VDIM = 128
BLOCK = 64
HEADS = 64
HALF_HEADS = 32
CAND = 384
TOK = 128
HALF = 8192
SLAB = 1024

offsets = (1, 2, 3, 4)
MESH = pl.DeviceIdType.MESH
NT = (((1,), (1,)), ((), ()))
TN = (((0,), (0,)), ((), ()))
VMEM = pl.BlockSpec(memory_space=pltpu.VMEM)
ANY = pl.BlockSpec(memory_space=pl.ANY)


class Place:
    def __init__(self):
        self.dp = lax.axis_index("dp")
        self.ctx = lax.axis_index("ctx")
        self.xh = self.dp // 4
        self.y = self.dp % 4
        self.core = self.ctx % 2
        self.chip = self.ctx // 2
        self.xl = self.chip % 2

    def sibling(self):
        return (self.dp, self.ctx + 1 - 2 * self.core)

    def in_ctx(self, chip, core):
        return (self.dp, chip * 2 + core)

    def side(self):
        return (self.dp, self.ctx + 2 - 4 * self.xl)

    def cross(self):
        return ((1 - self.xh) * 4 + self.y, self.ctx + 2 - 4 * self.xl)

    def ring(self, step):
        return (self.xh * 4 + (self.y + step) % 4, self.ctx)


def rdma(src, dst, send, recv, device):
    return pltpu.make_async_remote_copy(
        src_ref=src, dst_ref=dst, send_sem=send, recv_sem=recv, device_id=device,
        device_id_type=MESH,
    )


def greet(devices):
    barrier = pltpu.get_barrier_semaphore()
    for device in devices:
        pl.semaphore_signal(barrier, inc=1, device_id=device, device_id_type=MESH)
    pl.semaphore_wait(barrier, len(devices))


def gather_kernel(
    qn, qr, go, lt, own, box, bias, upw,
    qn2, qr2, go2, lt2, cand, bias2, weight,
    sib_rows, row_blk,
    loc, sib_s, sib_r, off_s, off_r, z_s, z_r, y_s, y_r, f_s, f_r, x_s, x_r, n_s, n_r,
):
    me = Place()
    core, chip = me.core, me.chip
    sib = me.sibling()
    peers = [me.in_ctx((chip + o) % 16, core) for o in range(1, 16)]
    peers += [me.in_ctx((chip + o) % 16, 1 - core) for o in range(16)]
    peers += [me.ring(1), me.ring(3), me.cross()]
    greet(peers)

    slab_col = lambda dp: pl.ds(pl.multiple_of(dp * SLAB, SLAB), SLAB)
    half_col = lambda k: pl.ds(pl.multiple_of(k * HALF + me.dp * SLAB, SLAB), SLAB)
    first = rdma(upw.at[:, half_col(1 - core)], sib_rows, sib_s.at[0], sib_r.at[0], sib)
    first.start()

    sends = []
    for m, o in enumerate(offsets):
        target = (me.ctx + o) % 32
        rows = pl.ds(pl.multiple_of((target % 2) * CAND + TOK + m * BLOCK, 64), BLOCK)
        for t in range(2):
            device = (me.dp, (target // 2) * 2 + t)
            landing = off_r.at[m * 2 + target % 2]
            cp = rdma(box.at[m], cand.at[rows, :], off_s.at[m * 2 + t], landing, device)
            if m == 0 and t == 0:
                pl.when(core == 0)(
                    pltpu.make_async_copy(box.at[m], cand.at[rows, :], landing).start)
                pl.when(core == 1)(cp.start)
                to_next = cp
            else:
                cp.start()
                sends.append(cp)

    qrow = pl.ds(pl.multiple_of(core * TOK, TOK), TOK)
    crow = pl.ds(pl.multiple_of(core * CAND, TOK), TOK)
    brow = pl.ds(pl.multiple_of(core * CAND, TOK), CAND)

    def col(k, width):
        return pl.ds(pl.multiple_of(k * width, width), width)

    pairs = [
        (lambda k: qn.at[:, col(k, 4096)], qn2.at[qrow, :]),
        (lambda k: qr.at[:, col(k, 2048)], qr2.at[qrow, :]),
        (lambda k: go.at[:, col(k, 4096)], go2.at[qrow, :]),
        (lambda k: lt.at[col(k, 32), :], lt2.at[core]),
        (lambda k: own, cand.at[crow, :]),
        (lambda k: bias, bias2.at[brow, :]),
    ]
    locals_ = []
    for i, (src, dst) in enumerate(pairs):
        cp = rdma(src(1 - core), dst, sib_s.at[1 + i], sib_r.at[1 + i], sib)
        cp.start()
        sends.append(cp)
        lc = pltpu.make_async_copy(src(core), dst, loc.at[i])
        lc.start()
        locals_.append(lc)

    first.wait_recv()
    mine = upw[:, half_col(core)].astype(jnp.float32)
    other = sib_rows[...].astype(jnp.float32)
    top = jnp.where(core == 0, mine, other)
    bottom = jnp.where(core == 0, other, mine)
    row_blk[...] = jnp.concatenate([top, bottom], axis=0).astype(jnp.bfloat16)
    my_slab = slab_col(me.dp)

    def chip_rows(c):
        return pl.ds(pl.multiple_of(c * 16, 16), 16)

    lc = pltpu.make_async_copy(row_blk, weight.at[chip_rows(chip), my_slab], loc.at[6])
    lc.start()
    locals_.append(lc)
    zs = []
    for o in range(1, 16):
        cp = rdma(row_blk, weight.at[chip_rows(chip), my_slab], z_s.at[o], z_r.at[o],
                  me.in_ctx((chip + o) % 16, core))
        cp.start()
        zs.append(cp)
    for o in range(1, 16):
        zs[o - 1].wait_recv()
    locals_.pop().wait()

    lo, hi, whole = pl.ds(0, 128), pl.ds(128, 128), pl.ds(0, 256)
    sent_half = pl.ds(pl.multiple_of(me.xl * 128, 128), 128)
    got_half = pl.ds(pl.multiple_of((1 - me.xl) * 128, 128), 128)
    blk = lambda xh, step: slab_col(xh * 4 + (me.y + step) % 4)

    def go_copy(rows, cols, s, r, device):
        cp = rdma(weight.at[rows, cols], weight.at[rows, cols], s, r, device)
        cp.start()
        sends.append(cp)

    def await_block(rows, cols, s, r):
        rdma(weight.at[rows, cols], weight.at[rows, cols], s, r, sib).wait_recv()

    def cross(step):
        go_copy(sent_half, blk(me.xh, step), x_s.at[step], x_r.at[step], me.cross())

    def relay(step):
        cols = blk(1 - me.xh, step)
        await_block(got_half, cols, x_s.at[step], x_r.at[step])
        go_copy(got_half, cols, n_s.at[step], n_r.at[step], me.side())

    go_copy(whole, my_slab, y_s.at[0], y_r.at[0], me.ring(1))
    go_copy(whole, my_slab, y_s.at[1], y_r.at[1], me.ring(3))
    cross(0)
    await_block(whole, blk(me.xh, 3), y_s.at[0], y_r.at[0])
    go_copy(lo, blk(me.xh, 3), f_s.at[0], f_r.at[0], me.ring(1))
    cross(3)
    await_block(whole, blk(me.xh, 1), y_s.at[1], y_r.at[1])
    go_copy(hi, blk(me.xh, 1), f_s.at[1], f_r.at[1], me.ring(3))
    cross(1)
    relay(0)
    await_block(lo, blk(me.xh, 2), f_s.at[0], f_r.at[0])
    await_block(hi, blk(me.xh, 2), f_s.at[1], f_r.at[1])
    cross(2)
    relay(3)
    relay(1)
    relay(2)
    for step in (0, 3, 1, 2):
        await_block(sent_half, blk(1 - me.xh, step), n_s.at[step], n_r.at[step])

    for cp in locals_:
        cp.wait()
    orow = pl.ds(pl.multiple_of((1 - core) * TOK, TOK), TOK)
    ocrow = pl.ds(pl.multiple_of((1 - core) * CAND, TOK), TOK)
    obrow = pl.ds(pl.multiple_of((1 - core) * CAND, TOK), CAND)
    landed = [qn2.at[orow, :], qr2.at[orow, :], go2.at[orow, :], lt2.at[1 - core],
              cand.at[ocrow, :], bias2.at[obrow, :]]
    for i, dst in enumerate(landed):
        rdma(dst, dst, sib_s.at[1 + i], sib_r.at[1 + i], sib).wait_recv()
    for m in range(4):
        for g in range(2):
            dst = cand.at[pl.ds(g * CAND + TOK + m * BLOCK, BLOCK), :]
            rdma(dst, dst, off_s.at[0], off_r.at[m * 2 + g], sib).wait_recv()
    first.wait_send()
    pl.when(core == 1)(to_next.wait_send)
    for cp in zs + sends:
        cp.wait_send()


def gather_call(qn, qr, go, lt, own, box, bias, upw):
    bf = jnp.bfloat16
    dma = pltpu.SemaphoreType.DMA
    return pl.pallas_call(
        gather_kernel,
        out_shape=(
            jax.ShapeDtypeStruct((2 * TOK, 4096), bf),
            jax.ShapeDtypeStruct((2 * TOK, 2048), bf),
            jax.ShapeDtypeStruct((2 * TOK, 4096), bf),
            jax.ShapeDtypeStruct((2, HALF_HEADS, TOK), jnp.float32),
            jax.ShapeDtypeStruct((2 * CAND, LAT + ROPE), bf),
            jax.ShapeDtypeStruct((2 * CAND, TOK), bf),
            jax.ShapeDtypeStruct((LAT, HALF), bf),
        ),
        in_specs=[ANY] * 7 + [VMEM],
        out_specs=(ANY,) * 7,
        scratch_shapes=[
            pltpu.VMEM((8, SLAB), bf),
            pltpu.VMEM((16, SLAB), bf),
            dma((7,)), dma((7,)), dma((7,)), dma((8,)), dma((8,)),
            dma((16,)), dma((16,)), dma((2,)), dma((2,)), dma((2,)), dma((2,)),
            dma((4,)), dma((4,)), dma((4,)), dma((4,)),
        ],
        compiler_params=pltpu.CompilerParams(collective_id=0, has_side_effects=True),
        name="gather_inputs",
    )(qn, qr, go, lt, own, box, bias, upw)


def dg(a, b, dims):
    return lax.dot_general(a, b, dims, preferred_element_type=jnp.float32)


def mm(a, b):
    return jnp.dot(a, b, preferred_element_type=jnp.float32)


SCALE = 1.0 / float(NOPE + ROPE) ** 0.5


def heads_kernel(
    qn, qr, go, lt, c, bias, w, gqn, gqr, dw, cg, rope_a, rope_b, ct, lat, rope_acc
):
    bf = jnp.bfloat16
    zero = jnp.zeros((2 * CAND, ROPE), bf)
    rp = c[:, LAT:]
    rope_a[...] = jnp.concatenate([rp, zero], axis=1)
    rope_b[...] = jnp.concatenate([zero, rp], axis=1)
    ct[...] = c[:, :LAT].T
    lat[...] = jnp.zeros_like(lat)
    rope_acc[...] = jnp.zeros_like(rope_acc)
    lane = lax.broadcasted_iota(jnp.int32, (CAND, 128), 1)
    z128 = jnp.zeros((TOK, 128), bf)

    @pl.loop(0, HALF_HEADS // 2)
    def _(p):
        rcol = pl.ds(pl.multiple_of(p * 128, 128), 128)
        whs, kvs = [], []
        for e in range(2):
            wh = w[:, pl.ds(pl.multiple_of(p * 512 + e * 256, 256), 256)]
            whs.append(wh)
            kvs.append(mm(c[:, :LAT], wh).astype(bf))
        kgs = [[None, None], [None, None]]
        for g in range(2):
            rows = slice(g * CAND, (g + 1) * CAND)
            qrow = slice(g * TOK, (g + 1) * TOK)
            qrp = qr[qrow, rcol]
            hcol = [pl.ds(pl.multiple_of(p * 256 + e * 128, 128), 128) for e in range(2)]
            gos = [go[qrow, hcol[e]] for e in range(2)]
            bd = jnp.concatenate(
                [jnp.concatenate([gos[0], z128], axis=1),
                 jnp.concatenate([z128, gos[1]], axis=1)], axis=0)
            vals = jnp.concatenate([kvs[0][rows, 128:], kvs[1][rows, 128:]], axis=1)
            dp_t = dg(vals, bd, NT)
            gr, rk, lows = None, [], []
            for e in range(2):
                rope = (rope_a if e == 0 else rope_b)[rows, :]
                kcat = jnp.concatenate([kvs[e][rows, :128], rope], axis=1)
                qcat = jnp.concatenate([qn[qrow, hcol[e]], qrp], axis=1)
                s_t = dg(kcat, qcat, NT)
                shift = bias[rows, :].astype(jnp.float32) - lt[g, pl.ds(p * 2 + e, 1), :]
                p_t = jnp.exp(s_t * SCALE + shift)
                d = dp_t[:, e * 128:(e + 1) * 128]
                rd = jnp.sum(p_t * d, axis=0, keepdims=True)
                sg = (p_t * (d - rd)).astype(bf)
                lows.append(p_t.astype(bf))
                gq = dg(sg, kcat, TN) * SCALE
                gqn[qrow, hcol[e]] = gq[:, :128].astype(bf)
                gr = gq[:, 128:] if gr is None else gr + gq[:, 128:]
                kg = mm(sg, qcat) * SCALE
                rk.append(kg[:, 128:])
                kgs[e][g] = kg[:, :128].astype(bf)
            gqr[qrow, rcol] = gr.astype(bf)
            vg = mm(jnp.concatenate(lows, axis=1), bd).astype(bf)
            for e in range(2):
                kgs[e][g] = jnp.concatenate([kgs[e][g], vg[:, e * 128:(e + 1) * 128]], axis=1)
            rope_acc[rows, :] += jnp.where(lane < ROPE, rk[0], rk[1])
        tot = None
        for e in range(2):
            kga = jnp.concatenate(kgs[e], axis=0)
            dw[:, pl.ds(pl.multiple_of(p * 512 + e * 256, 256), 256)] = mm(ct[...], kga)
            t = dg(kga, whs[e], NT)
            tot = t if tot is None else tot + t
        lat[...] += tot

    ra = rope_acc[...]
    cg[...] = jnp.concatenate([lat[...], ra[:, :ROPE] + ra[:, ROPE:]], axis=1)


def heads_call(qn, qr, go, lt, c, bias, w):
    bf = jnp.bfloat16
    return pl.pallas_call(
        heads_kernel,
        out_shape=(
            jax.ShapeDtypeStruct((2 * TOK, 4096), bf),
            jax.ShapeDtypeStruct((2 * TOK, 2048), bf),
            jax.ShapeDtypeStruct((LAT, HALF), jnp.float32),
            jax.ShapeDtypeStruct((2 * CAND, LAT + ROPE), jnp.float32),
        ),
        in_specs=[VMEM] * 7,
        out_specs=(VMEM,) * 4,
        scratch_shapes=[
            pltpu.VMEM((2 * CAND, 128), bf),
            pltpu.VMEM((2 * CAND, 128), bf),
            pltpu.VMEM((LAT, 2 * CAND), bf),
            pltpu.VMEM((2 * CAND, LAT), jnp.float32),
            pltpu.VMEM((2 * CAND, 128), jnp.float32),
        ],
        compiler_params=pltpu.CompilerParams(vmem_limit_bytes=56 << 20),
        name="heads",
    )(qn, qr, go, lt, c, bias, w)


ORDER = (2, 1, 3, 0)


def reduce_kernel(
    gqn, gqr, dw, cg,
    out_n, out_r, got, own2, out_w,
    acc, xsend, xrecv, csend, crecv, y2s, y2r, y1s, y1r, zbuf, fin,
    ld, loc, sib_s, sib_r, off_s, off_r, x_s, x_r, c_s, c_r, y2_s, y2_r, y1_s, y1_r,
    z_s, z_r, w_s, w_r,
):
    bf = jnp.bfloat16
    me = Place()
    core, chip = me.core, me.chip
    sib = me.sibling()
    peers = [me.in_ctx((chip + o) % 16, core) for o in range(1, 16)]
    peers += [me.in_ctx((chip + o) % 16, 1 - core) for o in range(16)]
    peers += [(r, chip * 2 + c) for o in range(1, 8) for c in range(2) for r in [(me.dp + o) % 8]]
    peers += [me.cross()]
    blk = lambda xh, step: pl.ds(
        pl.multiple_of((xh * 4 + (me.y + step) % 4) * SLAB, SLAB), SLAB)
    lo, hi = pl.ds(0, 128), pl.ds(128, 128)
    keep_half = pl.ds(pl.multiple_of(me.xl * 128, 128), 128)
    give_half = pl.ds(pl.multiple_of((1 - me.xl) * 128, 128), 128)

    loads = []
    for side in range(2):
        for i, step in enumerate(ORDER):
            cols = blk(1 - me.xh if side == 0 else me.xh, step)
            cp = pltpu.make_async_copy(dw.at[:, cols], acc.at[side * 4 + i], ld.at[side * 4 + i])
            cp.start()
            loads.append(cp)
    greet(peers)

    sends = []
    locals_ = []

    def send(src, dst, s, r, device):
        cp = rdma(src, dst, s, r, device)
        cp.start()
        sends.append(cp)
        return cp

    for i in range(4):
        loads[i].wait()
        xsend[i] = acc[i, give_half, :].astype(bf)
        send(xsend.at[i], xrecv.at[i], x_s.at[i], x_r.at[i], me.side())

    qrow = pl.ds(pl.multiple_of((1 - core) * TOK, TOK), TOK)
    mrow = pl.ds(pl.multiple_of(core * TOK, TOK), TOK)
    ncol = pl.ds(pl.multiple_of(core * 4096, 4096), 4096)
    rcol = pl.ds(pl.multiple_of(core * 2048, 2048), 2048)
    orow = pl.ds(pl.multiple_of((1 - core) * CAND, TOK), TOK)
    moff = pl.ds(pl.multiple_of(core * CAND, TOK), TOK)
    back = [
        send(gqn.at[qrow, :], out_n.at[:, ncol], sib_s.at[0], sib_r.at[0], sib),
        send(gqr.at[qrow, :], out_r.at[:, rcol], sib_s.at[1], sib_r.at[1], sib),
        send(cg.at[orow, :], own2.at[1], sib_s.at[2], sib_r.at[2], sib),
    ]
    for i, (src, dst) in enumerate([(gqn.at[mrow, :], out_n.at[:, ncol]),
                                    (gqr.at[mrow, :], out_r.at[:, rcol]),
                                    (cg.at[moff, :], own2.at[0])]):
        cp = pltpu.make_async_copy(src, dst, loc.at[i])
        cp.start()
        locals_.append(cp)
    for m, o in enumerate(offsets):
        for g in range(2):
            target = (chip * 2 + g + 32 - o) % 32
            src = cg.at[pl.ds(g * CAND + TOK + m * BLOCK, BLOCK), :]
            dst, landing = got.at[m * 2 + core], off_r.at[m * 2 + core]
            if m == 0 and g == 1:
                to_last = rdma(src, dst, off_s.at[1], landing, (me.dp, target))
                pl.when(core == 0)(pltpu.make_async_copy(src, dst, landing).start)
                pl.when(core == 1)(to_last.start)
            else:
                send(src, dst, off_s.at[m * 2 + g], landing, (me.dp, target))

    for i in range(4):
        rdma(xrecv.at[i], xrecv.at[i], x_s.at[i], x_r.at[i], sib).wait_recv()
        csend[i] = (acc[i, keep_half, :] + xrecv[i].astype(jnp.float32)).astype(bf)
        send(csend.at[i], crecv.at[i], c_s.at[i], c_r.at[i], me.cross())

    def crossed(i):
        loads[4 + i].wait()
        rdma(crecv.at[i], crecv.at[i], c_s.at[i], c_r.at[i], sib).wait_recv()
        acc[4 + i, give_half, :] += crecv[i].astype(jnp.float32)

    crossed(0)
    y2s[0] = acc[4, 0:128, :].astype(bf)
    send(y2s.at[0], y2r.at[0], y2_s.at[0], y2_r.at[0], me.ring(1))
    y2s[1] = acc[4, 128:256, :].astype(bf)
    send(y2s.at[1], y2r.at[1], y2_s.at[1], y2_r.at[1], me.ring(3))
    crossed(1)
    rdma(y2r.at[0], y2r.at[0], y2_s.at[0], y2_r.at[0], sib).wait_recv()
    y1s[0, 0:128, :] = (acc[5, 0:128, :] + y2r[0].astype(jnp.float32)).astype(bf)
    y1s[0, 128:256, :] = acc[5, 128:256, :].astype(bf)
    send(y1s.at[0], y1r.at[0], y1_s.at[0], y1_r.at[0], me.ring(1))
    crossed(2)
    rdma(y2r.at[1], y2r.at[1], y2_s.at[1], y2_r.at[1], sib).wait_recv()
    y1s[1, 0:128, :] = acc[6, 0:128, :].astype(bf)
    y1s[1, 128:256, :] = (acc[6, 128:256, :] + y2r[1].astype(jnp.float32)).astype(bf)
    send(y1s.at[1], y1r.at[1], y1_s.at[1], y1_r.at[1], me.ring(3))
    crossed(3)
    rdma(y1r.at[0], y1r.at[0], y1_s.at[0], y1_r.at[0], sib).wait_recv()
    rdma(y1r.at[1], y1r.at[1], y1_s.at[1], y1_r.at[1], sib).wait_recv()
    acc[7] = acc[7] + (y1r[0].astype(jnp.float32) + y1r[1].astype(jnp.float32))

    for o in range(1, 16):
        to = (chip + o) % 16
        rows = pl.ds(pl.multiple_of(to * 16, 16), 16)
        send(acc.at[7, rows, :], zbuf.at[o], z_s.at[o], z_r.at[o], me.in_ctx(to, core))
    total = acc[7, pl.ds(pl.multiple_of(chip * 16, 16), 16), :]
    for o in range(1, 16):
        rdma(zbuf.at[o], zbuf.at[o], z_s.at[o], z_r.at[o], sib).wait_recv()
        total = total + zbuf[o]
    fin[...] = total

    cols = pl.ds(pl.multiple_of(core * HALF + me.dp * SLAB, SLAB), SLAB)
    for o in range(8):
        r = (me.dp + o) % 8
        for f in range(2):
            if o == 0 and f == 0:
                continue
            c = core if f == 0 else 1 - core
            rows = pl.ds(pl.multiple_of(c * 8, 8), 8)
            send(fin.at[rows, :], out_w.at[:, cols], w_s.at[o * 2 + f], w_r.at[o * 2 + f],
                 (r, chip * 2 + c))
    cp = pltpu.make_async_copy(
        fin.at[pl.ds(pl.multiple_of(core * 8, 8), 8), :], out_w.at[:, cols], loc.at[3])
    cp.start()
    locals_.append(cp)
    for o in range(8):
        r = (me.dp + 8 - o) % 8
        for f in range(2):
            if o == 0 and f == 0:
                continue
            c = core if f == 0 else 1 - core
            dst = out_w.at[:, pl.ds(pl.multiple_of(c * HALF + r * SLAB, SLAB), SLAB)]
            rdma(dst, dst, w_s.at[0], w_r.at[o * 2 + f], sib).wait_recv()

    for m in range(4):
        for c in range(2):
            dst = got.at[m * 2 + c]
            rdma(dst, dst, off_s.at[0], off_r.at[m * 2 + c], sib).wait_recv()
    dsts = [out_n.at[:, pl.ds(pl.multiple_of((1 - core) * 4096, 4096), 4096)],
            out_r.at[:, pl.ds(pl.multiple_of((1 - core) * 2048, 2048), 2048)],
            own2.at[1]]
    for i, dst in enumerate(dsts):
        rdma(dst, dst, sib_s.at[i], sib_r.at[i], sib).wait_recv()
    for cp in locals_:
        cp.wait()
    pl.when(core == 1)(to_last.wait_send)
    for cp in sends:
        cp.wait_send()


def reduce_call(gqn, gqr, dw, cg):
    bf, f32 = jnp.bfloat16, jnp.float32
    dma = pltpu.SemaphoreType.DMA
    return pl.pallas_call(
        reduce_kernel,
        out_shape=(
            jax.ShapeDtypeStruct((TOK, HEADS * NOPE), bf),
            jax.ShapeDtypeStruct((TOK, HEADS * ROPE), bf),
            jax.ShapeDtypeStruct((8, BLOCK, LAT + ROPE), f32),
            jax.ShapeDtypeStruct((2, TOK, LAT + ROPE), f32),
            jax.ShapeDtypeStruct((8, 2 * HALF), f32),
        ),
        in_specs=[ANY] * 4,
        out_specs=(ANY,) * 5,
        scratch_shapes=[
            pltpu.VMEM((8, LAT, SLAB), f32),
            pltpu.VMEM((4, 128, SLAB), bf), pltpu.VMEM((4, 128, SLAB), bf),
            pltpu.VMEM((4, 128, SLAB), bf), pltpu.VMEM((4, 128, SLAB), bf),
            pltpu.VMEM((2, 128, SLAB), bf), pltpu.VMEM((2, 128, SLAB), bf),
            pltpu.VMEM((2, 256, SLAB), bf), pltpu.VMEM((2, 256, SLAB), bf),
            pltpu.VMEM((16, 16, SLAB), f32),
            pltpu.VMEM((16, SLAB), f32),
            dma((8,)), dma((4,)), dma((3,)), dma((3,)), dma((8,)), dma((8,)),
            dma((4,)), dma((4,)), dma((4,)), dma((4,)),
            dma((2,)), dma((2,)), dma((2,)), dma((2,)),
            dma((16,)), dma((16,)), dma((16,)), dma((16,)),
        ],
        compiler_params=pltpu.CompilerParams(
            collective_id=1, has_side_effects=True, vmem_limit_bytes=40 << 20),
        name="reduce_grads",
    )(gqn, gqr, dw, cg)


def key_bias(selection, offer_plan, group):
    ids = [group * 2, group * 2 + 1]
    for m, o in enumerate(offsets):
        source = group - o
        sender = jnp.maximum(source, 0)
        ids.append(jnp.where(source >= 0, sender * 2 + offer_plan[sender, m], -1))
    key_ids = jnp.stack(ids)
    query_ids = group * 2 + jnp.arange(2, dtype=jnp.int32)
    same = key_ids[:, None] == query_ids[None, :]
    picked = jnp.any(selection[None, :, :] == key_ids[:, None, None], axis=2)
    picked = picked & (key_ids >= 0)[:, None]
    inner = jnp.arange(BLOCK, dtype=jnp.int32)
    causal = inner[None, :] >= inner[:, None]
    ok = picked[:, None, :, None] | same[:, None, :, None] & causal[None, :, None, :]
    return jnp.where(ok.reshape(CAND, TOK), 0.0, -1e30).astype(jnp.bfloat16)


def shards(q_nope, q_rope, grad_out, log_total, kv_latent, up_weight, selected, offered):
    group = lax.axis_index("ctx")
    own = kv_latent[0]
    offer = offered[0, group]
    bias = key_bias(selected[0], offered[0], group)
    pick = (offer == 0)[:, None, None]
    box = jnp.where(pick, own[None, :BLOCK], own[None, BLOCK:])
    qn2, qr2, go2, lt2, cand, bias2, weight = gather_call(
        q_nope[0], q_rope[0], grad_out[0], log_total[0], own, box, bias, up_weight)
    gqn, gqr, dw, cg = heads_call(qn2, qr2, go2, lt2, cand, bias2, weight)
    out_n, out_r, got, own2, out_w = reduce_call(gqn, gqr, dw, cg)
    returned = got.reshape(4, 2, BLOCK, LAT + ROPE).sum(axis=1)
    first = jnp.where(pick, returned, 0.0).sum(axis=0)
    second = jnp.where(pick, 0.0, returned).sum(axis=0)
    grad_rows = own2[0] + own2[1] + jnp.concatenate([first, second], axis=0)
    return (out_n[None], out_r[None], grad_rows[None], out_w)


def solution(mesh):
    in_specs = (
        P("dp", "ctx", None),
        P("dp", "ctx", None),
        P("dp", "ctx", None),
        P("dp", None, "ctx"),
        P("dp", "ctx", None),
        P("ctx", None),
        P("dp", "ctx", None),
        P("dp", None, None),
    )
    out_specs = (P("dp", "ctx", None), P("dp", "ctx", None), P("dp", "ctx", None), P("ctx", None))
    return jax.shard_map(shards, mesh=mesh, in_specs=in_specs, out_specs=out_specs, check_vma=False)
```

time: 559 us -> 258 us (0.46); the launches traced: 552 us -> 258 us
  waiting for transfers between devices: 301 us -> 0 us
  Pallas kernels: 0 us -> 237 us
  matrix products: 128 us -> 0 us
  local copies, waits for them, and re-layouts: 67.3 us -> 14.5 us
  starting transfers between devices: 20.6 us -> 0 us
  between operations: 19.1 us -> 3.3 us
  other arithmetic: 15.1 us -> 3.06 us
    pallas_call x0 -> x3, Pallas kernels: none -> 237 us  [the longest x1 98.1 us: gather_call(): pl.pallas_call(gather_kernel, out_shape=(jax.ShapeDtypeStruct((2 * TOK, 4...]
    reduce_scatter x1 -> x0, waiting for transfers between devices: 164 us -> none  [shards(): lax.psum_scatter(lax.dot_general(latent_cols, key_grads, (((0,), (0,)), (...]
    dot_general x67 -> x0, matrix products: 128 us -> none  [the longest x8 18.6 us: head_backward(): jnp.einsum('hqk,khd->qhd', score_grads, key_part, preferred_element_type=...]
    psum x1 -> x0, waiting for transfers between devices: 85.3 us -> none  [shards(): grad_weight = lax.psum(shard_sum, 'dp')]
    all_gather x1 -> x0, waiting for transfers between devices: 44.4 us -> none  [shards(): weight = lax.all_gather(up_weight, 'ctx', axis=0, tiled=True)]
    ppermute x8 -> x0, starting transfers between devices: 20.5 us -> none  [from_behind(): lax.ppermute(value, axis, [(source, source + steps) for source in range(i...]
    reshape x1 -> x0, local copies, waits for them, and re-layouts: 20.5 us -> none  [regroup(): return array.reshape(length, groups, per_group, width).transpose(1, 0, 2, 3)]
    unnamed x18 -> x15, local copies, waits for them, and re-layouts: 22.3 us -> 10.7 us
  transfers between devices with their start and end apart: 11 -> 0, of which waited for: 4 -> 0; matrix products, arithmetic and copies ran while one was open for 6% -> 0% of each run, Pallas kernels for 0% -> 0%
where the time goes in v1:
time: 258 us
  Pallas kernels  237 us (92%)
  local copies, waits for them, and re-layouts  14.5 us (6%)
  between operations  3.3 us (1%)
  other arithmetic  3.06 us (1%)
    pallas_call x1, Pallas kernels, gather_call(): pl.pallas_call(gather_kernel, out_shape=(jax.ShapeDtypeStruct((2 * TOK, 4...  98.1 us
    pallas_call x1, Pallas kernels, reduce_call(): pl.pallas_call(reduce_kernel, out_shape=(jax.ShapeDtypeStruct((TOK, HEADS...  90.8 us
    pallas_call x1, Pallas kernels, heads_call(): pl.pallas_call(heads_kernel, out_shape=(jax.ShapeDtypeStruct((2 * TOK, 40...  47.9 us
    unnamed x15, local copies, waits for them, and re-layouts  10.7 us

profile of v1, /device:TPU:1, one launch (start us, length us, event | category | flops | bytes accessed | tf_op | source)
XLA Modules:
  0.0 257.6 jit_solution(1962379460224077063)
XLA Ops:
  0.7 0.9 fusion.1
  1.5 1.5 constant_dynamic-slice_fusion
  5.7 0.8 compare_reduce_fusion
  6.5 0.1 copy.19
  6.7 1.6 copy.16
  8.3 1.0 slice_bitcast_fusion.1
  9.4 0.1 copy.17
  9.5 0.1 copy.18
  9.6 0.8 broadcast_select_fusion.box
  10.4 0.3 fusion
  10.7 0.8 convert_element_type.6.bias
  11.5 98.1 %gather_inputs.1 = (bf16[256,4096]{1,0:T(8,128)(2,1)}, bf16[256,2048]{1,0:T(8,128)(2,1)}, bf16[256,4096]{1,0:T(8,128)(2,1)}, f32[2,32,128]{2,1,0:T(8,128)}, bf16...) custom-call(bf16[128,8192]{1,0:T(8,128)(2,1)} %bitcast.28, bf16[128,4096]{1,0:T(8,128)(2,1)} %bitcast.30, ...), custom_call_target="tpu_custom_call" | custom-call | tf_op jit(solution)/shard_map/gather_inputs/pallas_call | solution.py:216
  109.6 47.9 %heads.1 = (bf16[256,4096]{1,0:T(8,128)(2,1)}, bf16[256,2048]{1,0:T(8,128)(2,1)}, f32[256,8192]{1,0:T(8,128)}, f32[768,320]{1,0:T(8,128)}) custom-call(bf16[256,4096]{1,0:T(8,128)(2,1)} %get-tuple-element.20.qn, bf16[256,2048]{1,0:T(8,128)(2,1)} %get-tuple-element.21.qr, bf16[256,4096]{1,0:T(8,128)(2,1)} %get-tuple-element.22.go, ...), custom_call_target="tpu_custom_call" | custom-call | tf_op jit(solution)/shard_map/heads/pallas_call | solution.py:323
  157.5 1.6 copy-done
  159.1 1.3 copy-done.1
  160.3 1.2 copy-done.2
  161.6 90.8 %reduce_grads.1 = (bf16[128,8192]{1,0:T(8,128)(2,1)S(1)}, bf16[128,4096]{1,0:T(8,128)(2,1)S(1)}, f32[8,64,320]{2,1,0:T(8,128)S(1)}, f32[2,128,320]{2,1,0:T(8,128)S(1)}, f32[8,16384]{1,0:T(8,128)S(1)}) custom-call(bf16[256,4096]{1,0:T(8,128)(2,1)S(1)} %copy-done, bf16[256,2048]{1,0:T(8,128)(2,1)S(1)} %copy-done.2, f32[256,8192]{1,0:T(8,128)} %get-tuple-element.29.dw, ...), custom_call_target="tpu_custom_call" | custom-call | tf_op jit(solution)/shard_map/reduce_grads/pallas_call | solution.py:503
  252.4 0.7 copy-done.3
  253.1 0.1 select_reduce_fusion.1
  253.3 0.8 copy.20
  254.1 1.3 copy.24
  255.4 1.0 copy.25
  256.4 0.4 copy-done.4
  256.8 0.8 copy.26
  (13 shorter events, 0.3 us)
Async XLA Ops:
  157.5 1.6 copy-start
  159.1 1.3 copy-start.1
  160.3 1.2 copy-start.2
  252.3 0.8 copy-start.3
  255.4 1.4 copy-start.4

commit v2 on v0

v2 whole, which is shorter than its diff:
```python
import functools

import jax
import jax.numpy as jnp
from jax import lax
from jax.experimental import pallas as pl
from jax.experimental.pallas import tpu as pltpu
from jax.sharding import PartitionSpec as P

LAT = 256
ROPE = 64
NOPE = 128
VDIM = 128
BLOCK = 64
HEADS = 64
HALF_HEADS = 32
CAND = 384
TOK = 128
HALF = 8192
SLAB = 1024

offsets = (1, 2, 3, 4)
MESH = pl.DeviceIdType.MESH
NT = (((1,), (1,)), ((), ()))
TN = (((0,), (0,)), ((), ()))
VMEM = pl.BlockSpec(memory_space=pltpu.VMEM)
ANY = pl.BlockSpec(memory_space=pl.ANY)


class Place:
    def __init__(self):
        self.dp = lax.axis_index("dp")
        self.ctx = lax.axis_index("ctx")
        self.xh = self.dp // 4
        self.y = self.dp % 4
        self.core = self.ctx % 2
        self.chip = self.ctx // 2
        self.xl = self.chip % 2

    def sibling(self):
        return (self.dp, self.ctx + 1 - 2 * self.core)

    def in_ctx(self, chip, core):
        return (self.dp, chip * 2 + core)

    def side(self):
        return (self.dp, self.ctx + 2 - 4 * self.xl)

    def cross(self):
        return ((1 - self.xh) * 4 + self.y, self.ctx + 2 - 4 * self.xl)

    def ring(self, step):
        return (self.xh * 4 + (self.y + step) % 4, self.ctx)


def rdma(src, dst, send, recv, device):
    return pltpu.make_async_remote_copy(
        src_ref=src, dst_ref=dst, send_sem=send, recv_sem=recv, device_id=device,
        device_id_type=MESH,
    )


def greet(devices):
    barrier = pltpu.get_barrier_semaphore()
    for device in devices:
        pl.semaphore_signal(barrier, inc=1, device_id=device, device_id_type=MESH)
    pl.semaphore_wait(barrier, len(devices))


def dg(a, b, dims):
    return lax.dot_general(a, b, dims, preferred_element_type=jnp.float32)


def mm(a, b):
    return jnp.dot(a, b, preferred_element_type=jnp.float32)


SCALE = 1.0 / float(NOPE + ROPE) ** 0.5


UNITS = (
    ((0, 0), (0, 3), (0, 1), (1, 0), (0, 2), (1, 3), (1, 1), (1, 2)),
    ((1, 2), (1, 1), (1, 3), (1, 0), (0, 2), (0, 1), (0, 3), (0, 0)),
)
SLOT = {(f, u): f * 8 + i for f in range(2) for i, u in enumerate(UNITS[f])}
WIDE = SLAB // 2


class Sems:
    def __init__(self):
        self.at = {}
        self.count = 0

    def __call__(self, name, size=1):
        if name not in self.at:
            self.at[name] = self.count
            self.count += size
        return self.at[name]


NSEM = 256


def fused_kernel(
    qn, qr, go, lt, own, box, bias, upw,
    out_n, out_r, got, own2, out_w,
    qn2, qr2, go2, lt2, c, bias2, w, sib_rows, row_blk,
    gqn, gqr, cg, cgl, rope_a, rope_b, ct, lat, rope_acc,
    acc, xsend, xrecv, csend, crecv, y2s, y2r, y1s, y1r, zbuf, fin,
    ss, rs, ls,
):
    bf, f32 = jnp.bfloat16, jnp.float32
    me = Place()
    core, chip = me.core, me.chip
    sib = me.sibling()
    peers = [me.in_ctx((chip + o) % 16, core) for o in range(1, 16)]
    peers += [me.in_ctx((chip + o) % 16, 1 - core) for o in (0, 1, 2, 14, 15)]
    peers += [((me.dp + o) % 8, chip * 2 + k) for o in range(1, 8) for k in range(2)]
    peers += [me.cross()]

    chip_at = [(chip + o) % 16 for o in range(16)]
    y_at = [(me.y + o) % 4 for o in range(4)]

    sem = Sems()
    sends = []
    local = []

    def send(src, dst, name, device, land=None):
        at = sem(name)
        rdma(src(), dst(), ss.at[at], rs.at[at if land is None else land], device).start()
        sends.append((src, at))

    def got_it(ref, at):
        at = sem(at) if not isinstance(at, int) else at
        rdma(ref, ref, ss.at[at], rs.at[at], sib).wait_recv()

    def copy(src, dst):
        cp = pltpu.make_async_copy(src, dst, ls.at[len(local)])
        cp.start()
        local.append(cp)

    def rows_at(start, size, unit=8):
        return pl.ds(pl.multiple_of(start, unit), size)

    def col(k, width):
        return pl.ds(pl.multiple_of(k * width, width), width)

    def cols_of(f, side, step):
        xh = me.xh if side == 0 else 1 - me.xh
        return col((xh * 4 + y_at[step]) * 2 + f, WIDE)

    qrow, crow, brow = rows_at(core * TOK, TOK, TOK), rows_at(core * CAND, TOK, TOK), rows_at(
        core * CAND, CAND, TOK)
    pairs = [
        (lambda k: qn.at[:, col(k, 4096)], lambda k: qn2.at[rows_at(k * TOK, TOK, TOK), :]),
        (lambda k: qr.at[:, col(k, 2048)], lambda k: qr2.at[rows_at(k * TOK, TOK, TOK), :]),
        (lambda k: go.at[:, col(k, 4096)], lambda k: go2.at[rows_at(k * TOK, TOK, TOK), :]),
        (lambda k: lt.at[col(k, 32), :], lambda k: lt2.at[k]),
        (lambda k: own, lambda k: c.at[rows_at(k * CAND, TOK, TOK), :]),
        (lambda k: bias, lambda k: bias2.at[rows_at(k * CAND, CAND, TOK), :]),
    ]
    for src, dst in pairs:
        copy(src(core), dst(core))
    greet(peers)

    half_col = lambda k: pl.ds(pl.multiple_of(k * HALF + me.dp * SLAB, SLAB), SLAB)
    send(lambda: upw.at[:, half_col(1 - core)], lambda: sib_rows, "rows", sib)

    land0 = sem("offer_in", 8)
    for m, o in enumerate(offsets):
        target = (me.ctx + o) % 32
        place = rows_at((target % 2) * CAND + TOK + m * BLOCK, BLOCK, 64)
        for t in range(2):
            device = (me.dp, (target // 2) * 2 + t)
            land = land0 + m * 2 + target % 2
            if m == 0 and t == 0:
                at = sem("to_next")
                to_next = rdma(box.at[m], c.at[place, :], ss.at[at], rs.at[land], device)
                pl.when(core == 0)(
                    pltpu.make_async_copy(box.at[m], c.at[place, :], rs.at[land]).start)
                pl.when(core == 1)(to_next.start)
            else:
                send(lambda m=m: box.at[m], lambda place=place: c.at[place, :],
                     ("offer", m, t), device, land)
    for i, (src, dst) in enumerate(pairs):
        send(lambda src=src: src(1 - core), lambda dst=dst: dst(core), ("sib", i), sib)

    got_it(sib_rows, "rows")
    mine = upw[:, half_col(core)].astype(f32)
    other = sib_rows[...].astype(f32)
    top = jnp.where(core == 0, mine, other)
    bottom = jnp.where(core == 0, other, mine)
    row_blk[...] = jnp.concatenate([top, bottom], axis=0).astype(bf)
    my_rows = rows_at(chip * 16, 16, 16)
    for f in range(2):
        part = pl.ds(f * WIDE, WIDE)
        w[my_rows, cols_of(f, 0, 0)] = row_blk[:, part]
        for o in range(1, 16):
            send(lambda part=part: row_blk.at[:, part],
                 lambda f=f: w.at[my_rows, cols_of(f, 0, 0)],
                 ("z", f, o), me.in_ctx((chip + o) % 16, core))

    lo, hi, whole = pl.ds(0, 128), pl.ds(128, 128), pl.ds(0, 256)
    sent_half = rows_at(me.xl * 128, 128, 128)
    got_half = rows_at((1 - me.xl) * 128, 128, 128)

    def pass_on(rows, f, side, step, name, device):
        ref = lambda: w.at[rows, cols_of(f, side, step)]
        send(ref, ref, (name, f, step), device)

    def arrived(rows, f, side, step, name, as_step=None):
        got_it(w.at[rows, cols_of(f, side, step)], (name, f, step if as_step is None else as_step))

    def cross(f, step):
        pass_on(sent_half, f, 0, step, "cross", me.cross())

    def relay(f, step):
        arrived(got_half, f, 1, step, "cross")
        pass_on(got_half, f, 1, step, "side", me.side())

    def gather_a(f):
        for o in range(1, 16):
            ref = w.at[rows_at(chip_at[16 - o] * 16, 16, 16), cols_of(f, 0, 0)]
            got_it(ref, ("z", f, o))
        ref = lambda: w.at[whole, cols_of(f, 0, 0)]
        send(ref, ref, ("up", f), me.ring(1))
        send(ref, ref, ("down", f), me.ring(3))
        cross(f, 0)

    def gather_b(f):
        got_it(w.at[whole, cols_of(f, 0, 3)], ("up", f))
        ref3 = lambda: w.at[lo, cols_of(f, 0, 3)]
        send(ref3, ref3, ("up2", f), me.ring(1))
        cross(f, 3)
        got_it(w.at[whole, cols_of(f, 0, 1)], ("down", f))
        ref1 = lambda: w.at[hi, cols_of(f, 0, 1)]
        send(ref1, ref1, ("down2", f), me.ring(3))
        cross(f, 1)

    def gather_c(f):
        got_it(w.at[lo, cols_of(f, 0, 2)], ("up2", f))
        got_it(w.at[hi, cols_of(f, 0, 2)], ("down2", f))
        cross(f, 2)

    def side_done(f, step):
        arrived(sent_half, f, 1, step, "side")

    def reduce_x(f, step):
        at = f * 4 + step
        xsend[at] = acc[SLOT[f, (1, step)], sent_half, :].astype(bf)
        send(lambda: xsend.at[at], lambda: xrecv.at[at], ("rx", at), me.side())

    def reduce_cross(f, step):
        at = f * 4 + step
        got_it(xrecv.at[at], ("rx", at))
        csend[at] = (acc[SLOT[f, (1, step)], got_half, :] + xrecv[at].astype(f32)).astype(bf)
        send(lambda: csend.at[at], lambda: crecv.at[at], ("rc", at), me.cross())

    def crossed(f, step):
        at = f * 4 + step
        got_it(crecv.at[at], ("rc", at))
        acc[SLOT[f, (0, step)], sent_half, :] += crecv[at].astype(f32)

    def reduce_y2(f):
        crossed(f, 2)
        for i, step in enumerate((1, 3)):
            at = f * 2 + i
            y2s[at] = acc[SLOT[f, (0, 2)], i * 128:(i + 1) * 128, :].astype(bf)
            send(lambda at=at: y2s.at[at], lambda at=at: y2r.at[at], ("ry2", at), me.ring(step))

    def reduce_y1(f, i):
        step = (1, 3)[i]
        crossed(f, step)
        at = f * 2 + i
        got_it(y2r.at[at], ("ry2", at))
        slot = SLOT[f, (0, step)]
        near, far = slice(i * 128, (i + 1) * 128), slice((1 - i) * 128, (2 - i) * 128)
        y1s[at, near, :] = (acc[slot, near, :] + y2r[at].astype(f32)).astype(bf)
        y1s[at, far, :] = acc[slot, far, :].astype(bf)
        send(lambda: y1s.at[at], lambda: y1r.at[at], ("ry1", at), me.ring(step))

    def reduce_z(f):
        slot = SLOT[f, (0, 0)]
        crossed(f, 0)
        for i in range(2):
            got_it(y1r.at[f * 2 + i], ("ry1", f * 2 + i))
        acc[slot] = acc[slot] + (y1r[f * 2].astype(f32) + y1r[f * 2 + 1].astype(f32))
        for o in range(1, 16):
            send(lambda o=o: acc.at[slot, rows_at(chip_at[o] * 16, 16, 16), :],
                 lambda o=o: zbuf.at[f * 16 + o], ("rz", f, o), me.in_ctx(chip_at[o], core))

    def finish(f):
        total = acc[SLOT[f, (0, 0)], my_rows, :]
        for o in range(1, 16):
            got_it(zbuf.at[f * 16 + o], ("rz", f, o))
            total = total + zbuf[f * 16 + o]
        fin[f] = total
        for o in range(8):
            for k in range(2):
                if o == 0 and k == 0:
                    continue
                to = core if k == 0 else 1 - core
                send(lambda to=to: fin.at[f, rows_at(to * 8, 8), :], lambda: out_cols(f, core, me.dp),
                     ("w", f, o, k), ((me.dp + o) % 8, chip * 2 + to))

    def out_cols(f, k, r):
        return out_w.at[:, col((k * 8 + r) * 2 + f, WIDE)]

    before = {
        0: [lambda: gather_a(0)],
        1: [lambda: gather_b(0), lambda: relay(0, 0)],
        2: [lambda: gather_c(0), lambda: gather_a(1)],
        3: [lambda: relay(0, 3), lambda: side_done(0, 0)],
        4: [lambda: relay(0, 1), lambda: gather_b(1)],
        5: [lambda: reduce_x(0, 0), lambda: relay(0, 2), lambda: relay(1, 0),
            lambda: gather_c(1), lambda: side_done(0, 3)],
        6: [lambda: reduce_x(0, 3), lambda: reduce_cross(0, 0), lambda: relay(1, 3),
            lambda: side_done(0, 1)],
        7: [lambda: reduce_x(0, 1), lambda: relay(1, 1), lambda: relay(1, 2),
            lambda: side_done(0, 2)],
        8: [lambda: reduce_x(0, 2), lambda: reduce_cross(0, 3), lambda: side_done(1, 2)],
        9: [lambda: reduce_x(1, 2), lambda: reduce_cross(0, 1), lambda: side_done(1, 1)],
        10: [lambda: reduce_x(1, 1), lambda: reduce_cross(0, 2), lambda: side_done(1, 3)],
        11: [lambda: reduce_x(1, 3), lambda: reduce_cross(1, 2), lambda: side_done(1, 0)],
        12: [lambda: reduce_x(1, 0), lambda: reduce_cross(1, 1), lambda: reduce_y2(0)],
        13: [lambda: reduce_cross(1, 3), lambda: reduce_y2(1), lambda: reduce_y1(0, 0)],
        14: [lambda: reduce_cross(1, 0), lambda: reduce_y1(1, 0), lambda: reduce_y1(0, 1)],
        15: [lambda: reduce_y1(1, 1), lambda: reduce_z(0)],
    }

    for cp in local:
        cp.wait()
    for i, (_, dst) in enumerate(pairs):
        got_it(dst(1 - core), ("sib", i))
    for m in range(4):
        for g in range(2):
            got_it(c.at[pl.ds(g * CAND + TOK + m * BLOCK, BLOCK), :], land0 + m * 2 + g)
    zero = jnp.zeros((2 * CAND, ROPE), bf)
    rp = c[:, LAT:]
    rope_a[...] = jnp.concatenate([rp, zero], axis=1)
    rope_b[...] = jnp.concatenate([zero, rp], axis=1)
    ct[...] = c[:, :LAT].T
    lat[...] = jnp.zeros_like(lat)
    rope_acc[...] = jnp.zeros_like(rope_acc)
    lane = lax.broadcasted_iota(jnp.int32, (CAND, 128), 1)
    z128 = jnp.zeros((TOK, 128), bf)

    @pl.loop(0, 16)
    def _(s):
        for k, events in before.items():
            @pl.when(s == k)
            def _(events=events):
                for event in events:
                    event()
        side, step = [
            sum((s == SLOT[f, u]).astype(jnp.int32) * u[i] for f in range(2) for u in UNITS[f] if u[i])
            for i in range(2)]
        xh = me.xh + side - 2 * me.xh * side
        p = (xh * 4 + (me.y + step) % 4) * 2 + s // 8

        rcol = pl.ds(pl.multiple_of(p * 128, 128), 128)
        whs, kvs = [], []
        for e in range(2):
            wh = w[:, pl.ds(pl.multiple_of(p * 512 + e * 256, 256), 256)]
            whs.append(wh)
            kvs.append(mm(c[:, :LAT], wh).astype(bf))
        kgs = [[None, None], [None, None]]
        for g in range(2):
            rows = slice(g * CAND, (g + 1) * CAND)
            qs = slice(g * TOK, (g + 1) * TOK)
            qrp = qr2[qs, rcol]
            hcol = [pl.ds(pl.multiple_of(p * 256 + e * 128, 128), 128) for e in range(2)]
            gos = [go2[qs, hcol[e]] for e in range(2)]
            bd = jnp.concatenate(
                [jnp.concatenate([gos[0], z128], axis=1),
                 jnp.concatenate([z128, gos[1]], axis=1)], axis=0)
            vals = jnp.concatenate([kvs[0][rows, 128:], kvs[1][rows, 128:]], axis=1)
            dp_t = dg(vals, bd, NT)
            gr, rk, lows = None, [], []
            for e in range(2):
                rope = (rope_a if e == 0 else rope_b)[rows, :]
                kcat = jnp.concatenate([kvs[e][rows, :128], rope], axis=1)
                qcat = jnp.concatenate([qn2[qs, hcol[e]], qrp], axis=1)
                s_t = dg(kcat, qcat, NT)
                shift = bias2[rows, :].astype(f32) - lt2[g, pl.ds(p * 2 + e, 1), :]
                p_t = jnp.exp(s_t * SCALE + shift)
                d = dp_t[:, e * 128:(e + 1) * 128]
                rd = jnp.sum(p_t * d, axis=0, keepdims=True)
                sg = (p_t * (d - rd)).astype(bf)
                lows.append(p_t.astype(bf))
                gq = dg(sg, kcat, TN) * SCALE
                gqn[qs, hcol[e]] = gq[:, :128].astype(bf)
                gr = gq[:, 128:] if gr is None else gr + gq[:, 128:]
                kg = mm(sg, qcat) * SCALE
                rk.append(kg[:, 128:])
                kgs[e][g] = kg[:, :128].astype(bf)
            gqr[qs, rcol] = gr.astype(bf)
            vg = mm(jnp.concatenate(lows, axis=1), bd).astype(bf)
            for e in range(2):
                kgs[e][g] = jnp.concatenate([kgs[e][g], vg[:, e * 128:(e + 1) * 128]], axis=1)
            rope_acc[rows, :] += jnp.where(lane < ROPE, rk[0], rk[1])
        tot = None
        for e in range(2):
            kga = jnp.concatenate(kgs[e], axis=0)
            acc[s, :, e * 256:(e + 1) * 256] = mm(ct[...], kga)
            t = dg(kga, whs[e], NT)
            tot = t if tot is None else tot + t
        lat[...] += tot

    reduce_z(1)
    ra = rope_acc[...]
    full = jnp.concatenate([lat[...], ra[:, :ROPE] + ra[:, ROPE:]], axis=1)
    cg[...] = full
    cgl[...] = full.astype(bf)

    back0 = sem("back_in", 8)
    for m, o in enumerate(offsets):
        for g in range(2):
            target = (chip * 2 + g + 32 - o) % 32
            src = lambda m=m, g=g: cgl.at[pl.ds(g * CAND + TOK + m * BLOCK, BLOCK), :]
            dst = lambda m=m: got.at[m * 2 + core]
            land = back0 + m * 2 + core
            if m == 0 and g == 1:
                at = sem("to_last")
                to_last = rdma(src(), dst(), ss.at[at], rs.at[land], (me.dp, target))
                pl.when(core == 0)(pltpu.make_async_copy(src(), dst(), rs.at[land]).start)
                pl.when(core == 1)(to_last.start)
            else:
                send(src, dst, ("back", m, g), (me.dp, target), land)

    other_row = rows_at((1 - core) * TOK, TOK, TOK)
    ncol = lambda k: out_n.at[:, col(k, 4096)]
    rcol_ = lambda k: out_r.at[:, col(k, 2048)]
    send(lambda: gqn.at[other_row, :], lambda: ncol(core), "back_n", sib)
    send(lambda: gqr.at[other_row, :], lambda: rcol_(core), "back_r", sib)
    send(lambda: cg.at[rows_at((1 - core) * CAND, TOK, TOK), :], lambda: own2.at[1], "back_o", sib)
    first_late = len(local)
    copy(gqn.at[qrow, :], ncol(core))
    copy(gqr.at[qrow, :], rcol_(core))
    copy(cg.at[crow, :], own2.at[0])

    finish(0)
    finish(1)
    for f in range(2):
        copy(fin.at[f, rows_at(core * 8, 8), :], out_cols(f, core, me.dp))
    got_it(ncol(1 - core), "back_n")
    got_it(rcol_(1 - core), "back_r")
    got_it(own2.at[1], "back_o")
    for m in range(4):
        for k in range(2):
            got_it(got.at[m * 2 + k], back0 + m * 2 + k)
    for f in range(2):
        for o in range(8):
            for k in range(2):
                if o == 0 and k == 0:
                    continue
                who = core if k == 0 else 1 - core
                got_it(out_cols(f, who, (me.dp + 8 - o) % 8), ("w", f, o, k))
    for cp in local[first_late:]:
        cp.wait()
    pl.when(core == 1)(to_next.wait_send)
    pl.when(core == 1)(to_last.wait_send)
    for src, at in sends:
        rdma(src(), src(), ss.at[at], rs.at[at], sib).wait_send()
    assert sem.count <= NSEM, sem.count


def fused_call(qn, qr, go, lt, own, box, bias, upw):
    bf, f32 = jnp.bfloat16, jnp.float32
    dma = pltpu.SemaphoreType.DMA
    v = pltpu.VMEM
    return pl.pallas_call(
        fused_kernel,
        out_shape=(
            jax.ShapeDtypeStruct((TOK, HEADS * NOPE), bf),
            jax.ShapeDtypeStruct((TOK, HEADS * ROPE), bf),
            jax.ShapeDtypeStruct((8, BLOCK, LAT + ROPE), bf),
            jax.ShapeDtypeStruct((2, TOK, LAT + ROPE), f32),
            jax.ShapeDtypeStruct((8, 2 * HALF), f32),
        ),
        in_specs=[ANY] * 7 + [VMEM],
        out_specs=(ANY,) * 5,
        scratch_shapes=[
            v((2 * TOK, 4096), bf), v((2 * TOK, 2048), bf), v((2 * TOK, 4096), bf),
            v((2, HALF_HEADS, TOK), f32), v((2 * CAND, LAT + ROPE), bf), v((2 * CAND, TOK), bf),
            v((LAT, HALF), bf), v((8, SLAB), bf), v((16, SLAB), bf),
            v((2 * TOK, 4096), bf), v((2 * TOK, 2048), bf),
            v((2 * CAND, LAT + ROPE), f32), v((2 * CAND, LAT + ROPE), bf),
            v((2 * CAND, 128), bf), v((2 * CAND, 128), bf), v((LAT, 2 * CAND), bf),
            v((2 * CAND, LAT), f32), v((2 * CAND, 128), f32),
            v((16, LAT, WIDE), f32),
            v((8, 128, WIDE), bf), v((8, 128, WIDE), bf), v((8, 128, WIDE), bf),
            v((8, 128, WIDE), bf),
            v((4, 128, WIDE), bf), v((4, 128, WIDE), bf),
            v((4, 256, WIDE), bf), v((4, 256, WIDE), bf),
            v((32, 16, WIDE), f32), v((2, 16, WIDE), f32),
            dma((NSEM,)), dma((NSEM,)), dma((16,)),
        ],
        compiler_params=pltpu.CompilerParams(
            collective_id=0, has_side_effects=True, vmem_limit_bytes=56 << 20),
        name="fused_backward",
    )(qn, qr, go, lt, own, box, bias, upw)


def key_bias(selection, offer_plan, group):
    ids = [group * 2, group * 2 + 1]
    for m, o in enumerate(offsets):
        source = group - o
        sender = jnp.maximum(source, 0)
        ids.append(jnp.where(source >= 0, sender * 2 + offer_plan[sender, m], -1))
    key_ids = jnp.stack(ids)
    query_ids = group * 2 + jnp.arange(2, dtype=jnp.int32)
    same = key_ids[:, None] == query_ids[None, :]
    picked = jnp.any(selection[None, :, :] == key_ids[:, None, None], axis=2)
    picked = picked & (key_ids >= 0)[:, None]
    inner = jnp.arange(BLOCK, dtype=jnp.int32)
    causal = inner[None, :] >= inner[:, None]
    ok = picked[:, None, :, None] | same[:, None, :, None] & causal[None, :, None, :]
    return jnp.where(ok.reshape(CAND, TOK), 0.0, -1e30).astype(jnp.bfloat16)


def shards(q_nope, q_rope, grad_out, log_total, kv_latent, up_weight, selected, offered):
    group = lax.axis_index("ctx")
    own = kv_latent[0]
    offer = offered[0, group]
    bias = key_bias(selected[0], offered[0], group)
    pick = (offer == 0)[:, None, None]
    box = jnp.where(pick, own[None, :BLOCK], own[None, BLOCK:])
    out_n, out_r, got, own2, out_w = fused_call(
        q_nope[0], q_rope[0], grad_out[0], log_total[0], own, box, bias, up_weight)
    returned = got.astype(jnp.float32).reshape(4, 2, BLOCK, LAT + ROPE).sum(axis=1)
    first = jnp.where(pick, returned, 0.0).sum(axis=0)
    second = jnp.where(pick, 0.0, returned).sum(axis=0)
    grad_rows = own2[0] + own2[1] + jnp.concatenate([first, second], axis=0)
    return (out_n[None], out_r[None], grad_rows[None], out_w)


def solution(mesh):
    in_specs = (
        P("dp", "ctx", None),
        P("dp", "ctx", None),
        P("dp", "ctx", None),
        P("dp", None, "ctx"),
        P("dp", "ctx", None),
        P("ctx", None),
        P("dp", "ctx", None),
        P("dp", None, None),
    )
    out_specs = (P("dp", "ctx", None), P("dp", "ctx", None), P("dp", "ctx", None), P("ctx", None))
    return jax.shard_map(shards, mesh=mesh, in_specs=in_specs, out_specs=out_specs, check_vma=False)
```

time: 559 us -> 153 us (0.27); the launches traced: 552 us -> 152 us
  waiting for transfers between devices: 301 us -> 0 us
  Pallas kernels: 0 us -> 133 us
  matrix products: 128 us -> 0 us
  local copies, waits for them, and re-layouts: 67.3 us -> 10.2 us
  starting transfers between devices: 20.6 us -> 0 us
  between operations: 19.1 us -> 3.35 us
  other arithmetic: 15.1 us -> 5.29 us
    reduce_scatter x1 -> x0, waiting for transfers between devices: 164 us -> none  [shards(): lax.psum_scatter(lax.dot_general(latent_cols, key_grads, (((0,), (0,)), (...]
    pallas_call x0 -> x1, Pallas kernels: none -> 133 us  [fused_call(): pl.pallas_call(fused_kernel, out_shape=(jax.ShapeDtypeStruct((TOK, HEADS...]
    dot_general x67 -> x0, matrix products: 128 us -> none  [the longest x8 18.6 us: head_backward(): jnp.einsum('hqk,khd->qhd', score_grads, key_part, preferred_element_type=...]
    psum x1 -> x0, waiting for transfers between devices: 85.3 us -> none  [shards(): grad_weight = lax.psum(shard_sum, 'dp')]
    all_gather x1 -> x0, waiting for transfers between devices: 44.4 us -> none  [shards(): weight = lax.all_gather(up_weight, 'ctx', axis=0, tiled=True)]
    ppermute x8 -> x0, starting transfers between devices: 20.5 us -> none  [from_behind(): lax.ppermute(value, axis, [(source, source + steps) for source in range(i...]
    reshape x1 -> x0, local copies, waits for them, and re-layouts: 20.5 us -> none  [regroup(): return array.reshape(length, groups, per_group, width).transpose(1, 0, 2, 3)]
    unnamed x18 -> x11, local copies, waits for them, and re-layouts: 22.3 us -> 6.57 us
  transfers between devices with their start and end apart: 11 -> 0, of which waited for: 4 -> 0; matrix products, arithmetic and copies ran while one was open for 6% -> 0% of each run, Pallas kernels for 0% -> 0%
where the time goes in v2:
time: 153 us; the launch traced here: 152 us
  Pallas kernels  133 us (87%)
  local copies, waits for them, and re-layouts  10.2 us (7%)
  other arithmetic  5.29 us (3%)
  between operations  3.35 us (2%)
    pallas_call x1, Pallas kernels, fused_call(): pl.pallas_call(fused_kernel, out_shape=(jax.ShapeDtypeStruct((TOK, HEADS...  133 us
    unnamed x11, local copies, waits for them, and re-layouts  6.57 us

profile of v2, /device:TPU:1, one launch (start us, length us, event | category | flops | bytes accessed | tf_op | source)
XLA Modules:
  0.0 152.1 jit_solution(9851847120447715293)
XLA Ops:
  0.6 1.4 constant_dynamic-slice_fusion
  4.7 0.1 stack.27
  4.8 0.8 compare_reduce_fusion
  5.6 0.1 copy.19
  5.7 0.1 broadcast_compare_fusion
  5.8 0.3 fusion
  6.1 0.8 convert_element_type.7.bias
  6.9 0.9 fusion.1
  7.8 1.1 slice_bitcast_fusion.1
  8.9 0.1 copy.17
  9.0 0.1 copy.18
  9.1 0.8 broadcast_select_fusion.box
  9.8 1.6 %copy.16 = bf16[1,128,320]{2,1,0:T(8,128)(2,1)} copy(bf16[1,128,320]{1,2,0:T(8,128)(2,1)} %param.12) | data formatting | bytes 163840 | tf_op args[4]
  11.5 133.2 %fused_backward.1 = (bf16[128,8192]{1,0:T(8,128)(2,1)}, bf16[128,4096]{1,0:T(8,128)(2,1)}, bf16[8,64,320]{2,1,0:T(8,128)(2,1)}, f32[2,128,320]{2,1,0:T(8,128)}, f32[8,16384]{1,0:T(8,128)}) custom-call(bf16[128,8192]{1,0:T(8,128)(2,1)} %bitcast.27, bf16[128,4096]{1,0:T(8,128)(2,1)} %bitcast.31, bf16[128,8192]{1,0:T(8,128)(2,1)} %bitcast.28, ...), custom_call_target="tpu_custom_call" | custom-call | tf_op jit(solution)/shard_map/fused_backward/pallas_call | solution.py:472
  144.7 0.0 copy-start
  144.7 1.2 convert_reduce_fusion
  146.0 0.1 select_reduce_fusion.1
  146.1 1.1 maximum_add_fusion
  147.1 0.8 copy.20
  147.9 1.3 copy.24
  149.3 0.6 copy-done.1
  149.9 1.0 copy.25
  150.9 0.4 copy-done.2
  151.3 0.8 copy.26
  (7 shorter events, 0.0 us)
Async XLA Ops:
  144.7 3.2 %copy-start = (bf16[128,8192]{1,0:T(8,128)(2,1)S(1)}, bf16[128,8192]{1,0:T(8,128)(2,1)}, u32[]{:S(2)}) copy-start(bf16[128,8192]{1,0:T(8,128)(2,1)} %get-tuple-element.9) | copy-start | bytes 6291460
  147.9 2.0 %copy-start.1 = (bf16[128,4096]{1,0:T(8,128)(2,1)S(1)}, bf16[128,4096]{1,0:T(8,128)(2,1)}, u32[]{:S(2)}) copy-start(bf16[128,4096]{1,0:T(8,128)(2,1)} %get-tuple-element.10) | copy-start | bytes 3145732
  149.9 1.4 copy-start.2

commit v3 on v2

v3 whole, which is shorter than its diff:
```python
import functools

import jax
import jax.numpy as jnp
from jax import lax
from jax.experimental import pallas as pl
from jax.experimental.pallas import tpu as pltpu
from jax.sharding import PartitionSpec as P

LAT = 256
ROPE = 64
NOPE = 128
VDIM = 128
BLOCK = 64
HEADS = 64
HALF_HEADS = 32
CAND = 384
TOK = 128
HALF = 8192
SLAB = 1024

offsets = (1, 2, 3, 4)
MESH = pl.DeviceIdType.MESH
NT = (((1,), (1,)), ((), ()))
TN = (((0,), (0,)), ((), ()))
VMEM = pl.BlockSpec(memory_space=pltpu.VMEM)
ANY = pl.BlockSpec(memory_space=pl.ANY)


class Place:
    def __init__(self):
        self.dp = lax.axis_index("dp")
        self.ctx = lax.axis_index("ctx")
        self.xh = self.dp // 4
        self.y = self.dp % 4
        self.core = self.ctx % 2
        self.chip = self.ctx // 2
        self.xl = self.chip % 2
        self.z = self.chip // 2

    def sibling(self):
        return (self.dp, self.ctx + 1 - 2 * self.core)

    def in_ctx(self, chip, core):
        return (self.dp, chip * 2 + core)

    def side(self):
        return (self.dp, self.ctx + 2 - 4 * self.xl)

    def along_z(self, step):
        return (self.dp, (self.ctx + 4 * step) % 32)

    def cross(self):
        return ((1 - self.xh) * 4 + self.y, self.ctx + 2 - 4 * self.xl)

    def ring(self, step):
        return (self.xh * 4 + (self.y + step) % 4, self.ctx)


def rdma(src, dst, send, recv, device):
    return pltpu.make_async_remote_copy(
        src_ref=src, dst_ref=dst, send_sem=send, recv_sem=recv, device_id=device,
        device_id_type=MESH,
    )


def signal_peers(devices):
    barrier = pltpu.get_barrier_semaphore()
    for device in devices:
        pl.semaphore_signal(barrier, inc=1, device_id=device, device_id_type=MESH)
    return barrier


def dg(a, b, dims):
    return lax.dot_general(a, b, dims, preferred_element_type=jnp.float32)


def mm(a, b):
    return jnp.dot(a, b, preferred_element_type=jnp.float32)


SCALE = 1.0 / float(NOPE + ROPE) ** 0.5


PLAN = (
    ("cross", 0, 0), ("along_y", 0), ("unit", 0, 0, 0), ("along_z", 1, 2), ("relay", 0, 0),
    ("up", 0), ("cross", 0, 1), ("down", 0), ("cross", 0, 3), ("unit", 0, 0, 3),
    ("unit", 0, 0, 1), ("cross", 0, 2), ("relay", 0, 1), ("along_z", 1, 3), ("unit", 0, 0, 2),
    ("relay", 0, 3), ("unit", 0, 1, 0), ("relay", 0, 2), ("unit", 0, 1, 1), ("along_z", 1, 4),
    ("unit", 0, 1, 3), ("add_x", 0, 3), ("unit", 0, 1, 2), ("add_x", 0, 2), ("add_x", 0, 1),
    ("unit", 1, 1, 2), ("unit", 1, 1, 0), ("add_cross", 0, 2), ("add_x", 1, 2), ("unit", 1, 1, 3),
    ("add_cross", 0, 3), ("add_cross", 0, 1), ("add_x", 1, 3), ("add_x", 0, 0), ("add_y2", 0),
    ("add_cross", 1, 2), ("unit", 1, 0, 2), ("unit", 1, 1, 1), ("add_y1", 0, 1), ("add_y1", 0, 0),
    ("add_x", 1, 1), ("add_cross", 0, 0), ("add_x", 1, 0), ("add_cross", 1, 3), ("unit", 1, 0, 1),
    ("add_y2", 1), ("add_cross", 1, 1), ("unit", 1, 0, 3), ("add_z", 0), ("add_y1", 1, 1),
    ("add_y1", 1, 0), ("add_cross", 1, 0), ("unit", 1, 0, 0), ("add_z", 1), ("add_side", 0),
    ("finish", 0), ("add_side", 1), ("finish", 1),
)
UNITS = [op[1:] for op in PLAN if op[0] == "unit"]
SLOT = {u: i for i, u in enumerate(UNITS)}
WIDE = SLAB // 2
LONG = HALF // 2


class Sems:
    def __init__(self):
        self.at = {}
        self.count = 0

    def __call__(self, name, size=1):
        if name not in self.at:
            self.at[name] = self.count
            self.count += size
        return self.at[name]


NSEM = 256


def fused_kernel(
    selected, offered, qn, qr, go, lt, own_t, upw,
    out_n, out_r, out_l, out_w,
    own, box, qn2, qr2, go2, lt2, c, bias2, w, in_slab, in_long, stage,
    gqn, gqr, cg, cgl, got, own2, rope_a, rope_b, ct, lat, rope_acc,
    acc, xsend, xrecv, csend, crecv, y2s, y2r, y1s, y1r, zbuf, part, side_in, fin,
    ss, rs, ls,
):
    bf, f32 = jnp.bfloat16, jnp.float32
    me = Place()
    core, chip = me.core, me.chip
    sib = me.sibling()
    chip_at = [(chip + o) % 16 for o in range(16)]
    y_at = [(me.y + o) % 4 for o in range(4)]
    z_at = [(me.z + o) % 8 for o in range(8)]
    peers = [sib] + [me.in_ctx(chip_at[o], k) for o in (1, 2, 14, 15) for k in range(2)]
    peers += [(me.dp, (z_at[o] * 2 + me.xl) * 2 + core) for o in range(2, 7)]
    peers += [((me.dp + o) % 8, chip * 2 + k) for o in range(1, 8) for k in range(2)]
    peers += [me.cross()]
    barrier = signal_peers(peers)

    sem = Sems()
    sends = []
    local = []
    seen = set()

    def send(src, dst, name, device, land=None):
        at = sem(name)
        rdma(src(), dst(), ss.at[at], rs.at[at if land is None else land], device).start()
        sends.append((src, at))

    def got_it(ref, name):
        if name not in seen:
            seen.add(name)
            at = name if isinstance(name, int) else sem(name)
            rdma(ref, ref, ss.at[at], rs.at[at], sib).wait_recv()

    def copy(src, dst):
        cp = pltpu.make_async_copy(src, dst, ls.at[len(local)])
        cp.start()
        local.append(cp)

    def rows_at(start, size, unit=8):
        return pl.ds(pl.multiple_of(start, unit), size)

    def col(k, width):
        return pl.ds(pl.multiple_of(k * width, width), width)

    def cols_of(f, side, step):
        xh = me.xh if side == 0 else 1 - me.xh
        return col(f * 8 + xh * 4 + y_at[step], WIDE)

    def rows_of(k):
        return rows_at(k * TOK, TOK, TOK)

    def crows_of(k, size):
        return rows_at(k * CAND, size, TOK)

    qrow, crow = rows_of(core), crows_of(core, TOK)
    pairs = [
        (lambda k: qn.at[:, col(k, 4096)], lambda k: qn2.at[rows_of(k), :]),
        (lambda k: qr.at[:, col(k, 2048)], lambda k: qr2.at[rows_of(k), :]),
        (lambda k: go.at[:, col(k, 4096)], lambda k: go2.at[rows_of(k), :]),
        (lambda k: lt.at[col(k, 32), :], lambda k: lt2.at[k]),
    ]
    for src, dst in pairs:
        copy(src(core), dst(core))

    group = me.ctx
    latent = own_t[...].astype(f32).T
    own[...] = latent.astype(bf)
    c[crow, :] = latent.astype(bf)
    offer = [offered[group, m] for m in range(4)]
    for m in range(4):
        box[m] = jnp.where(offer[m] == 0, latent[:BLOCK], latent[BLOCK:]).astype(bf)
    ids = [group * 2, group * 2 + 1]
    for m, o in enumerate(offsets):
        source = group - o
        sender = jnp.maximum(source, 0)
        ids.append(jnp.where(source >= 0, sender * 2 + offered[sender, m], -1))
    lane64 = lax.broadcasted_iota(jnp.int32, (BLOCK, TOK), 1)
    inner = lax.broadcasted_iota(jnp.int32, (BLOCK, TOK), 0)
    for k in range(6):
        cols = []
        for q in range(2):
            hit = (selected[q, 0] == ids[k]) | (selected[q, 1] == ids[k]) | (selected[q, 2] == ids[k])
            off = jnp.where(hit & (ids[k] >= 0), 0.0, -1e30).astype(f32)
            if k == q:
                place = lane64 - q * BLOCK
                cols.append(jnp.where(place >= inner, 0.0, jnp.broadcast_to(off, (BLOCK, TOK))))
            else:
                cols.append(jnp.broadcast_to(off, (BLOCK, TOK)))
        bias2[rows_at(core * CAND + k * BLOCK, BLOCK, 64), :] = jnp.where(
            lane64 < BLOCK, cols[0], cols[1]).astype(bf)
    pl.semaphore_wait(barrier, len(peers))

    near = [sib, me.side(), (me.dp, me.ctx + 2 - 4 * me.xl + 1 - 2 * core)]
    near_core = [1 - core, core, 1 - core]
    near_at = [me.xl * 2 + 1 - core, (1 - me.xl) * 2 + core, (1 - me.xl) * 2 + 1 - core]

    def slab_in(k):
        return upw.at[:, col(k * 16 + me.dp, WIDE)]

    def long_in(k):
        return upw.at[:, col(k * 2 + 1, LONG)]

    for i in range(3):
        send(lambda i=i: slab_in(near_core[i]), lambda i=i: in_slab.at[i], ("slab", i), near[i])
    for i in range(3):
        send(lambda i=i: long_in(near_core[i]), lambda i=i: in_long.at[i], ("long", i), near[i])

    land0 = sem("offer_in", 8)
    for m, o in enumerate(offsets):
        target = (me.ctx + o) % 32
        place = rows_at((target % 2) * CAND + TOK + m * BLOCK, BLOCK, 64)
        for t in range(2):
            device = (me.dp, (target // 2) * 2 + t)
            land = land0 + m * 2 + target % 2
            if m == 0 and t == 0:
                at = sem("to_next")
                to_next = rdma(box.at[m], c.at[place, :], ss.at[at], rs.at[land], device)
                pl.when(core == 0)(
                    pltpu.make_async_copy(box.at[m], c.at[place, :], rs.at[land]).start)
                pl.when(core == 1)(to_next.start)
            else:
                send(lambda m=m: box.at[m], lambda place=place: c.at[place, :],
                     ("offer", m, t), device, land)
    shared = [(lambda k: own, lambda k: c.at[crows_of(k, TOK), :]),
              (lambda k: bias2.at[crows_of(1 - k, CAND), :], lambda k: bias2.at[crows_of(k, CAND), :])]
    for i, (src, dst) in enumerate(pairs + shared):
        send(lambda src=src: src(1 - core), lambda dst=dst: dst(core), ("sib", i), sib)

    my_rows = rows_at(me.z * 32, 32, 32)
    zrows = lambda o: rows_at(z_at[o % 8] * 32, 32, 32)
    at_z = lambda o: (me.dp, (z_at[o % 8] * 2 + me.xl) * 2 + core)

    def assemble(arrived, mine, width, name):
        stage[rows_at((me.xl * 2 + core) * 8, 8), 0:width] = mine.astype(f32)
        for i in range(3):
            got_it(arrived.at[i], (name, i))
            stage[rows_at(near_at[i] * 8, 8), 0:width] = arrived[i].astype(f32)
        return stage[:, 0:width].astype(bf)

    w[my_rows, cols_of(0, 0, 0)] = assemble(
        in_slab, upw[:, col(core * 16 + me.dp, WIDE)], WIDE, "slab")
    for o in range(1, 8):
        ref = lambda: w.at[my_rows, cols_of(0, 0, 0)]
        send(ref, ref, ("z", o), at_z(o))
    w[my_rows, LONG:] = assemble(in_long, upw[:, col(core * 2 + 1, LONG)], LONG, "long")

    lo, hi, whole = pl.ds(0, 128), pl.ds(128, 128), pl.ds(0, 256)
    sent_half = rows_at(me.xl * 128, 128, 128)
    got_half = rows_at((1 - me.xl) * 128, 128, 128)
    full_long = pl.ds(LONG, LONG)
    quarters = [pl.ds(LONG, LONG // 2), pl.ds(LONG + LONG // 2, LONG // 2)]

    def ring_ref(n, way):
        rows = zrows(8 - (n - 1) if way == 0 else n - 1)
        return w.at[rows, full_long if n < 4 else quarters[way]]

    def ring_in(n, way):
        rows = zrows(8 - n if way == 0 else n)
        return w.at[rows, full_long if n < 4 else quarters[way]]

    def along_z(f, n):
        for way in range(2):
            if n > 1:
                got_it(ring_in(n - 1, way), ("ring", n - 1, way))
            ref = lambda way=way: ring_ref(n, way)
            send(ref, ref, ("ring", n, way), at_z(1 if way == 0 else 7))

    along_z(1, 1)

    def weight_part(rows, side, step, name):
        got_it(w.at[rows, cols_of(0, side, step)], name)

    def need_block(f, side, step):
        if f == 1:
            for n in range(1, 5):
                for way in range(2):
                    got_it(ring_in(n, way), ("ring", n, way))
        elif side == 1:
            weight_part(got_half, 1, step, ("cross", step))
            weight_part(sent_half, 1, step, ("side", step))
        elif step == 0:
            for o in range(1, 8):
                got_it(w.at[zrows(8 - o), cols_of(0, 0, 0)], ("z", o))
        elif step == 2:
            weight_part(lo, 0, 2, "up2")
            weight_part(hi, 0, 2, "down2")
        else:
            weight_part(whole, 0, step, "up" if step == 3 else "down")

    def pass_on(rows, side, step, name, device):
        ref = lambda: w.at[rows, cols_of(0, side, step)]
        send(ref, ref, name, device)

    def along_y(f):
        need_block(0, 0, 0)
        pass_on(whole, 0, 0, "up", me.ring(1))
        pass_on(whole, 0, 0, "down", me.ring(3))

    def cross(f, step):
        need_block(0, 0, step)
        pass_on(sent_half, 0, step, ("cross", step), me.cross())

    def up(f):
        need_block(0, 0, 3)
        pass_on(lo, 0, 3, "up2", me.ring(1))

    def down(f):
        need_block(0, 0, 1)
        pass_on(hi, 0, 1, "down2", me.ring(3))

    def relay(f, step):
        weight_part(got_half, 1, step, ("cross", step))
        pass_on(got_half, 1, step, ("side", step), me.side())

    def add_x(f, step):
        at = f * 4 + step
        xsend[at] = acc[SLOT[f, 1, step], sent_half, :].astype(bf)
        send(lambda: xsend.at[at], lambda: xrecv.at[at], ("rx", at), me.side())

    def add_cross(f, step):
        at = f * 4 + step
        got_it(xrecv.at[at], ("rx", at))
        csend[at] = (acc[SLOT[f, 1, step], got_half, :] + xrecv[at].astype(f32)).astype(bf)
        send(lambda: csend.at[at], lambda: crecv.at[at], ("rc", at), me.cross())

    def crossed(f, step):
        at = f * 4 + step
        got_it(crecv.at[at], ("rc", at))
        acc[SLOT[f, 0, step], sent_half, :] += crecv[at].astype(f32)

    def add_y2(f):
        crossed(f, 2)
        for i, step in enumerate((1, 3)):
            at = f * 2 + i
            y2s[at] = acc[SLOT[f, 0, 2], i * 128:(i + 1) * 128, :].astype(bf)
            send(lambda at=at: y2s.at[at], lambda at=at: y2r.at[at], ("ry2", at), me.ring(step))

    def add_y1(f, i):
        step = (1, 3)[i]
        crossed(f, step)
        at = f * 2 + i
        got_it(y2r.at[at], ("ry2", at))
        slot = SLOT[f, 0, step]
        near_half, far = slice(i * 128, (i + 1) * 128), slice((1 - i) * 128, (2 - i) * 128)
        y1s[at, near_half, :] = (acc[slot, near_half, :] + y2r[at].astype(f32)).astype(bf)
        y1s[at, far, :] = acc[slot, far, :].astype(bf)
        send(lambda: y1s.at[at], lambda: y1r.at[at], ("ry1", at), me.ring(step))

    def add_z(f):
        slot = SLOT[f, 0, 0]
        crossed(f, 0)
        for i in range(2):
            got_it(y1r.at[f * 2 + i], ("ry1", f * 2 + i))
        acc[slot] = acc[slot] + (y1r[f * 2].astype(f32) + y1r[f * 2 + 1].astype(f32))
        for o in range(1, 8):
            send(lambda o=o: acc.at[slot, zrows(o), :], lambda o=o: zbuf.at[f * 8 + o],
                 ("rz", f, o), at_z(o))

    def add_side(f):
        total = acc[SLOT[f, 0, 0], my_rows, :]
        for o in range(1, 8):
            got_it(zbuf.at[f * 8 + o], ("rz", f, o))
            total = total + zbuf[f * 8 + o]
        part[f] = total
        send(lambda: part.at[f, rows_at((1 - me.xl) * 16, 16, 16), :], lambda: side_in.at[f],
             ("pair", f), me.side())

    def finish(f):
        got_it(side_in.at[f], ("pair", f))
        fin[f] = part[f, rows_at(me.xl * 16, 16, 16), :] + side_in[f]
        for o in range(8):
            for k in range(2):
                if o == 0 and k == 0:
                    continue
                to = core if k == 0 else 1 - core
                send(lambda to=to: fin.at[f, rows_at(to * 8, 8), :], lambda: out_cols(f, core, me.dp),
                     ("w", f, o, k), ((me.dp + o) % 8, chip * 2 + to))

    def out_cols(f, k, r):
        return out_w.at[:, col(k * 16 + f * 8 + r, WIDE)]

    actions = dict(
        along_y=along_y, along_z=along_z, cross=cross, up=up, down=down, relay=relay, add_x=add_x,
        add_cross=add_cross, add_y2=add_y2, add_y1=add_y1, add_z=add_z, add_side=add_side,
        finish=finish, unit=need_block)
    before, events = [], []
    for op in PLAN:
        events.append(op)
        if op[0] == "unit":
            before.append(events)
            events = []
    after = events

    def act(ops):
        for name, *where in ops:
            actions[name](*where)

    for cp in local:
        cp.wait()
    for i, (_, dst) in enumerate(pairs + shared):
        got_it(dst(1 - core), ("sib", i))
    for m in range(4):
        for g in range(2):
            got_it(c.at[pl.ds(g * CAND + TOK + m * BLOCK, BLOCK), :], land0 + m * 2 + g)
    zero = jnp.zeros((2 * CAND, ROPE), bf)
    rp = c[:, LAT:]
    rope_a[...] = jnp.concatenate([rp, zero], axis=1)
    rope_b[...] = jnp.concatenate([zero, rp], axis=1)
    ct[...] = c[:, :LAT].T
    lat[...] = jnp.zeros_like(lat)
    rope_acc[...] = jnp.zeros_like(rope_acc)
    lane = lax.broadcasted_iota(jnp.int32, (CAND, 128), 1)
    z128 = jnp.zeros((TOK, 128), bf)

    @pl.loop(0, 16)
    def _(s):
        for k, ops in enumerate(before):
            @pl.when(s == k)
            def _(ops=ops):
                act(ops)
        half, side, step = [
            sum((s == k).astype(jnp.int32) * u[i] for k, u in enumerate(UNITS) if u[i])
            for i in range(3)]
        xh = me.xh + side - 2 * me.xh * side
        p = half * 8 + xh * 4 + (me.y + step) % 4

        rcol = pl.ds(pl.multiple_of(p * 128, 128), 128)
        whs, kvs = [], []
        for e in range(2):
            wh = w[:, pl.ds(pl.multiple_of(p * 512 + e * 256, 256), 256)]
            whs.append(wh)
            kvs.append(mm(c[:, :LAT], wh).astype(bf))
        kgs = [[None, None], [None, None]]
        for g in range(2):
            rows = slice(g * CAND, (g + 1) * CAND)
            qs = slice(g * TOK, (g + 1) * TOK)
            qrp = qr2[qs, rcol]
            hcol = [pl.ds(pl.multiple_of(p * 256 + e * 128, 128), 128) for e in range(2)]
            gos = [go2[qs, hcol[e]] for e in range(2)]
            bd = jnp.concatenate(
                [jnp.concatenate([gos[0], z128], axis=1),
                 jnp.concatenate([z128, gos[1]], axis=1)], axis=0)
            vals = jnp.concatenate([kvs[0][rows, 128:], kvs[1][rows, 128:]], axis=1)
            dp_t = dg(vals, bd, NT)
            gr, rk, lows = None, [], []
            for e in range(2):
                rope = (rope_a if e == 0 else rope_b)[rows, :]
                kcat = jnp.concatenate([kvs[e][rows, :128], rope], axis=1)
                qcat = jnp.concatenate([qn2[qs, hcol[e]], qrp], axis=1)
                s_t = dg(kcat, qcat, NT)
                shift = bias2[rows, :].astype(f32) - lt2[g, pl.ds(p * 2 + e, 1), :]
                p_t = jnp.exp(s_t * SCALE + shift)
                d = dp_t[:, e * 128:(e + 1) * 128]
                rd = jnp.sum(p_t * d, axis=0, keepdims=True)
                sg = (p_t * (d - rd)).astype(bf)
                lows.append(p_t.astype(bf))
                gq = dg(sg, kcat, TN) * SCALE
                gqn[qs, hcol[e]] = gq[:, :128].astype(bf)
                gr = gq[:, 128:] if gr is None else gr + gq[:, 128:]
                kg = mm(sg, qcat) * SCALE
                rk.append(kg[:, 128:])
                kgs[e][g] = kg[:, :128].astype(bf)
            gqr[qs, rcol] = gr.astype(bf)
            vg = mm(jnp.concatenate(lows, axis=1), bd).astype(bf)
            for e in range(2):
                kgs[e][g] = jnp.concatenate([kgs[e][g], vg[:, e * 128:(e + 1) * 128]], axis=1)
            rope_acc[rows, :] += jnp.where(lane < ROPE, rk[0], rk[1])
        tot = None
        for e in range(2):
            kga = jnp.concatenate(kgs[e], axis=0)
            acc[s, :, e * 256:(e + 1) * 256] = mm(ct[...], kga)
            t = dg(kga, whs[e], NT)
            tot = t if tot is None else tot + t
        lat[...] += tot

    last = after.index(("add_z", 1)) + 1
    act(after[:last])
    ra = rope_acc[...]
    full = jnp.concatenate([lat[...], ra[:, :ROPE] + ra[:, ROPE:]], axis=1)
    cg[...] = full
    cgl[...] = full.astype(bf)

    back0 = sem("back_in", 8)
    for m, o in enumerate(offsets):
        for g in range(2):
            target = (chip * 2 + g + 32 - o) % 32
            src = lambda m=m, g=g: cgl.at[pl.ds(g * CAND + TOK + m * BLOCK, BLOCK), :]
            dst = lambda m=m: got.at[m * 2 + core]
            land = back0 + m * 2 + core
            if m == 0 and g == 1:
                at = sem("to_last")
                to_last = rdma(src(), dst(), ss.at[at], rs.at[land], (me.dp, target))
                pl.when(core == 0)(pltpu.make_async_copy(src(), dst(), rs.at[land]).start)
                pl.when(core == 1)(to_last.start)
            else:
                send(src, dst, ("back", m, g), (me.dp, target), land)

    ncol = lambda k: out_n.at[:, col(k, 4096)]
    rcol_ = lambda k: out_r.at[:, col(k, 2048)]
    send(lambda: cg.at[crows_of(1 - core, TOK), :], lambda: own2, "back_o", sib)
    send(lambda: gqn.at[rows_of(1 - core), :], lambda: ncol(core), "back_n", sib)
    send(lambda: gqr.at[rows_of(1 - core), :], lambda: rcol_(core), "back_r", sib)
    first_late = len(local)
    copy(gqn.at[qrow, :], ncol(core))
    copy(gqr.at[qrow, :], rcol_(core))

    act(after[last:-2])

    got_it(own2, "back_o")
    total = cg[crow, :] + own2[...]
    first, second = total[:BLOCK], total[BLOCK:]
    for m in range(4):
        for k in range(2):
            got_it(got.at[m * 2 + k], back0 + m * 2 + k)
        rows = got[m * 2].astype(f32) + got[m * 2 + 1].astype(f32)
        nil = jnp.zeros_like(rows)
        first = first + jnp.where(offer[m] == 0, rows, nil)
        second = second + jnp.where(offer[m] == 0, nil, rows)
    out_l[0:BLOCK, :] = first
    out_l[BLOCK:TOK, :] = second

    act(after[-2:])
    for f in range(2):
        copy(fin.at[f, rows_at(core * 8, 8), :], out_cols(f, core, me.dp))
    got_it(ncol(1 - core), "back_n")
    got_it(rcol_(1 - core), "back_r")
    for f in range(2):
        for o in range(8):
            for k in range(2):
                if o == 0 and k == 0:
                    continue
                who = core if k == 0 else 1 - core
                got_it(out_cols(f, who, (me.dp + 8 - o) % 8), ("w", f, o, k))
    for cp in local[first_late:]:
        cp.wait()
    pl.when(core == 1)(to_next.wait_send)
    pl.when(core == 1)(to_last.wait_send)
    for src, at in sends:
        rdma(src(), src(), ss.at[at], rs.at[at], sib).wait_send()
    assert sem.count <= NSEM, sem.count


def fused_call(selected, offered, qn, qr, go, lt, own_t, upw):
    bf, f32 = jnp.bfloat16, jnp.float32
    dma = pltpu.SemaphoreType.DMA
    v = pltpu.VMEM
    smem = pl.BlockSpec(memory_space=pltpu.SMEM)
    return pl.pallas_call(
        fused_kernel,
        out_shape=(
            jax.ShapeDtypeStruct((TOK, HEADS * NOPE), bf),
            jax.ShapeDtypeStruct((TOK, HEADS * ROPE), bf),
            jax.ShapeDtypeStruct((TOK, LAT + ROPE), f32),
            jax.ShapeDtypeStruct((8, 2 * HALF), f32),
        ),
        in_specs=[smem, smem] + [ANY] * 4 + [VMEM, VMEM],
        out_specs=(ANY, ANY, VMEM, ANY),
        scratch_shapes=[
            v((TOK, LAT + ROPE), bf), v((4, BLOCK, LAT + ROPE), bf),
            v((2 * TOK, 4096), bf), v((2 * TOK, 2048), bf), v((2 * TOK, 4096), bf),
            v((2, HALF_HEADS, TOK), f32), v((2 * CAND, LAT + ROPE), bf), v((2 * CAND, TOK), bf),
            v((LAT, HALF), bf), v((3, 8, WIDE), bf), v((3, 8, LONG), bf), v((32, LONG), f32),
            v((2 * TOK, 4096), bf), v((2 * TOK, 2048), bf),
            v((2 * CAND, LAT + ROPE), f32), v((2 * CAND, LAT + ROPE), bf),
            v((8, BLOCK, LAT + ROPE), bf), v((TOK, LAT + ROPE), f32),
            v((2 * CAND, 128), bf), v((2 * CAND, 128), bf), v((LAT, 2 * CAND), bf),
            v((2 * CAND, LAT), f32), v((2 * CAND, 128), f32),
            v((16, LAT, WIDE), f32),
            v((8, 128, WIDE), bf), v((8, 128, WIDE), bf), v((8, 128, WIDE), bf),
            v((8, 128, WIDE), bf),
            v((4, 128, WIDE), bf), v((4, 128, WIDE), bf),
            v((4, 256, WIDE), bf), v((4, 256, WIDE), bf),
            v((16, 32, WIDE), f32), v((2, 32, WIDE), f32), v((2, 16, WIDE), f32),
            v((2, 16, WIDE), f32),
            dma((NSEM,)), dma((NSEM,)), dma((16,)),
        ],
        compiler_params=pltpu.CompilerParams(
            collective_id=0, has_side_effects=True, vmem_limit_bytes=56 << 20),
        name="fused_backward",
    )(selected, offered, qn, qr, go, lt, own_t, upw)


def shards(q_nope, q_rope, grad_out, log_total, kv_latent, up_weight, selected, offered):
    out_n, out_r, out_l, out_w = fused_call(
        selected[0], offered[0], q_nope[0], q_rope[0], grad_out[0], log_total[0], kv_latent[0].T,
        up_weight)
    return (out_n[None], out_r[None], out_l[None], out_w)


def solution(mesh):
    in_specs = (
        P("dp", "ctx", None),
        P("dp", "ctx", None),
        P("dp", "ctx", None),
        P("dp", None, "ctx"),
        P("dp", "ctx", None),
        P("ctx", None),
        P("dp", "ctx", None),
        P("dp", None, None),
    )
    out_specs = (P("dp", "ctx", None), P("dp", "ctx", None), P("dp", "ctx", None), P("ctx", None))
    return jax.shard_map(shards, mesh=mesh, in_specs=in_specs, out_specs=out_specs, check_vma=False)
```

time: 153 us -> 130 us (0.85)
  Pallas kernels: 133 us -> 121 us
  other arithmetic: 5.29 us -> 0 us
  between operations: 3.35 us -> 0.64 us
  local copies, waits for them, and re-layouts: 10.2 us -> 8.06 us
    pallas_call x1, Pallas kernels: 133 us -> 121 us  [fused_call(): pl.pallas_call(fused_kernel, out_shape=(jax.ShapeDtypeStruct((TOK, HEADS...]
    unnamed x11 -> x8, local copies, waits for them, and re-layouts: 6.57 us -> 6.69 us
where the time goes in v3:
time: 130 us
  Pallas kernels  121 us (93%)
  local copies, waits for them, and re-layouts  8.06 us (6%)
    pallas_call x1, Pallas kernels, fused_call(): pl.pallas_call(fused_kernel, out_shape=(jax.ShapeDtypeStruct((TOK, HEADS...  121 us
    unnamed x8, local copies, waits for them, and re-layouts  6.69 us

profile of v3, /device:TPU:1, one launch (start us, length us, event | category | flops | bytes accessed | tf_op | source)
XLA Modules:
  0.0 129.8 jit_solution(10858498729143142341)
XLA Ops:
  0.6 1.4 %copy.12.offered = s32[32,4]{1,0:T(8,128)} copy(s32[32,4]{0,1:T(4,128)} %bitcast.20) | data formatting | bytes 1024 | tf_op jit(solution)/shard_map/squeeze | solution.py:608
  2.0 121.1 %fused_backward.1 = (bf16[128,8192]{1,0:T(8,128)(2,1)}, bf16[128,4096]{1,0:T(8,128)(2,1)}, f32[128,320]{1,0:T(8,128)}, f32[8,16384]{1,0:T(8,128)}) custom-call(s32[2,3]{1,0:T(2,128)} %bitcast.21, s32[32,4]{1,0:T(8,128)} %copy.12.offered, bf16[128,8192]{1,0:T(8,128)(2,1)} %bitcast.12, bf16[128,4096]{1,0:T(8,128)(2,1)} %bitcast.16, ...), custom_call_target="tpu_custom_call" | custom-call | tf_op jit(solution)/shard_map/fused_backward/pallas_call | solution.py:571
  123.1 1.7 %copy.13 = f32[1,128,320]{1,2,0:T(8,128)} copy(f32[1,128,320]{2,1,0:T(8,128)} %bitcast.17) | data formatting | bytes 327680
  124.8 0.0 copy-start
  124.9 0.0 copy-start.1
  124.9 3.2 %copy.17 = bf16[1,128,8192]{2,1,0:T(8,128)(2,1)} copy(bf16[1,128,8192]{2,1,0:T(8,128)(2,1)} %bitcast.14) | data formatting | bytes 4194304
  128.1 0.0 copy-done
  128.1 1.0 copy.18
  129.0 0.0 copy-done.1
  129.0 0.8 copy.19
Async XLA Ops:
  124.8 3.2 %copy-start = (bf16[128,4096]{1,0:T(8,128)(2,1)S(1)}, bf16[128,4096]{1,0:T(8,128)(2,1)}, u32[]{:S(2)}) copy-start(bf16[128,4096]{1,0:T(8,128)(2,1)} %get-tuple-element.9) | copy-start | bytes 3145732
  124.9 4.2 %copy-start.1 = (f32[8,16384]{1,0:T(8,128)S(1)}, f32[8,16384]{1,0:T(8,128)}, u32[]{:S(2)}) copy-start(f32[8,16384]{1,0:T(8,128)} %get-tuple-element.23) | copy-start | bytes 1572868

commit v4 on v3

--- a/solution.py
+++ b/solution.py
@@ -83,17 +83,17 @@
 
 
 PLAN = (
-    ("cross", 0, 0), ("along_y", 0), ("unit", 0, 0, 0), ("along_z", 1, 2), ("relay", 0, 0),
-    ("up", 0), ("cross", 0, 1), ("down", 0), ("cross", 0, 3), ("unit", 0, 0, 3),
-    ("unit", 0, 0, 1), ("cross", 0, 2), ("relay", 0, 1), ("along_z", 1, 3), ("unit", 0, 0, 2),
-    ("relay", 0, 3), ("unit", 0, 1, 0), ("relay", 0, 2), ("unit", 0, 1, 1), ("along_z", 1, 4),
-    ("unit", 0, 1, 3), ("add_x", 0, 3), ("unit", 0, 1, 2), ("add_x", 0, 2), ("add_x", 0, 1),
-    ("unit", 1, 1, 2), ("unit", 1, 1, 0), ("add_cross", 0, 2), ("add_x", 1, 2), ("unit", 1, 1, 3),
-    ("add_cross", 0, 3), ("add_cross", 0, 1), ("add_x", 1, 3), ("add_x", 0, 0), ("add_y2", 0),
-    ("add_cross", 1, 2), ("unit", 1, 0, 2), ("unit", 1, 1, 1), ("add_y1", 0, 1), ("add_y1", 0, 0),
-    ("add_x", 1, 1), ("add_cross", 0, 0), ("add_x", 1, 0), ("add_cross", 1, 3), ("unit", 1, 0, 1),
-    ("add_y2", 1), ("add_cross", 1, 1), ("unit", 1, 0, 3), ("add_z", 0), ("add_y1", 1, 1),
-    ("add_y1", 1, 0), ("add_cross", 1, 0), ("unit", 1, 0, 0), ("add_z", 1), ("add_side", 0),
+    ("cross", 0, 0), ("along_y", 0), ("relay", 0, 0), ("unit", 0, 0, 0), ("cross", 0, 1),
+    ("cross", 0, 3), ("down", 0), ("up", 0), ("along_z", 1, 2), ("unit", 0, 0, 1),
+    ("unit", 0, 0, 3), ("cross", 0, 2), ("relay", 0, 1), ("unit", 0, 1, 0), ("relay", 0, 3),
+    ("along_z", 1, 3), ("unit", 0, 0, 2), ("relay", 0, 2), ("unit", 0, 1, 1), ("add_x", 0, 1),
+    ("unit", 0, 1, 3), ("along_z", 1, 4), ("unit", 0, 1, 2), ("add_x", 0, 2), ("add_x", 0, 3),
+    ("add_cross", 0, 1), ("add_x", 0, 0), ("unit", 1, 1, 2), ("add_x", 1, 2), ("add_cross", 0, 2),
+    ("unit", 1, 1, 1), ("unit", 1, 1, 0), ("add_y2", 0), ("add_cross", 0, 3), ("add_cross", 0, 0),
+    ("unit", 1, 1, 3), ("add_x", 1, 1), ("add_x", 1, 3), ("add_x", 1, 0), ("add_cross", 1, 2),
+    ("add_y1", 0, 0), ("add_y1", 0, 1), ("unit", 1, 0, 2), ("add_cross", 1, 1), ("unit", 1, 0, 1),
+    ("add_cross", 1, 3), ("add_y2", 1), ("unit", 1, 0, 3), ("add_z", 0), ("add_cross", 1, 0),
+    ("add_y1", 1, 0), ("add_y1", 1, 1), ("unit", 1, 0, 0), ("add_z", 1), ("add_side", 0),
     ("finish", 0), ("add_side", 1), ("finish", 1),
 )
 UNITS = [op[1:] for op in PLAN if op[0] == "unit"]
@@ -122,7 +122,7 @@
     out_n, out_r, out_l, out_w,
     own, box, qn2, qr2, go2, lt2, c, bias2, w, in_slab, in_long, stage,
     gqn, gqr, cg, cgl, got, own2, rope_a, rope_b, ct, lat, rope_acc,
-    acc, xsend, xrecv, csend, crecv, y2s, y2r, y1s, y1r, zbuf, part, side_in, fin,
+    acc, xsend, xrecv, csend, crecv, y2s, y2r, y1s, y1r, zbuf, part, side_in, low, low_in, fin,
     ss, rs, ls,
 ):
     bf, f32 = jnp.bfloat16, jnp.float32
@@ -132,8 +132,8 @@
     chip_at = [(chip + o) % 16 for o in range(16)]
     y_at = [(me.y + o) % 4 for o in range(4)]
     z_at = [(me.z + o) % 8 for o in range(8)]
-    peers = [sib] + [me.in_ctx(chip_at[o], k) for o in (1, 2, 14, 15) for k in range(2)]
-    peers += [(me.dp, (z_at[o] * 2 + me.xl) * 2 + core) for o in range(2, 7)]
+    peers = [(me.dp, (me.ctx + o) % 32) for o in (1, 2, 3, 4, 28, 29, 30, 31)]
+    peers += [me.in_ctx(chip_at[o], core) for o in range(3, 14)]
     peers += [((me.dp + o) % 8, chip * 2 + k) for o in range(1, 8) for k in range(2)]
     peers += [me.cross()]
     barrier = signal_peers(peers)
@@ -143,15 +143,15 @@
     local = []
     seen = set()
 
-    def send(src, dst, name, device, land=None):
+    def send(src, dst, name, device):
         at = sem(name)
-        rdma(src(), dst(), ss.at[at], rs.at[at if land is None else land], device).start()
+        rdma(src(), dst(), ss.at[at], rs.at[at], device).start()
         sends.append((src, at))
 
     def got_it(ref, name):
         if name not in seen:
             seen.add(name)
-            at = name if isinstance(name, int) else sem(name)
+            at = sem(name)
             rdma(ref, ref, ss.at[at], rs.at[at], sib).wait_recv()
 
     def copy(src, dst):
@@ -189,14 +189,14 @@
     latent = own_t[...].astype(f32).T
     own[...] = latent.astype(bf)
     c[crow, :] = latent.astype(bf)
-    offer = [offered[group, m] for m in range(4)]
+    offer = [offered[m, group] for m in range(4)]
     for m in range(4):
         box[m] = jnp.where(offer[m] == 0, latent[:BLOCK], latent[BLOCK:]).astype(bf)
     ids = [group * 2, group * 2 + 1]
     for m, o in enumerate(offsets):
         source = group - o
         sender = jnp.maximum(source, 0)
-        ids.append(jnp.where(source >= 0, sender * 2 + offered[sender, m], -1))
+        ids.append(jnp.where(source >= 0, sender * 2 + offered[m, sender], -1))
     lane64 = lax.broadcasted_iota(jnp.int32, (BLOCK, TOK), 1)
     inner = lax.broadcasted_iota(jnp.int32, (BLOCK, TOK), 0)
     for k in range(6):
@@ -228,26 +228,17 @@
     for i in range(3):
         send(lambda i=i: long_in(near_core[i]), lambda i=i: in_long.at[i], ("long", i), near[i])
 
-    land0 = sem("offer_in", 8)
     for m, o in enumerate(offsets):
-        target = (me.ctx + o) % 32
-        place = rows_at((target % 2) * CAND + TOK + m * BLOCK, BLOCK, 64)
-        for t in range(2):
-            device = (me.dp, (target // 2) * 2 + t)
-            land = land0 + m * 2 + target % 2
-            if m == 0 and t == 0:
-                at = sem("to_next")
-                to_next = rdma(box.at[m], c.at[place, :], ss.at[at], rs.at[land], device)
-                pl.when(core == 0)(
-                    pltpu.make_async_copy(box.at[m], c.at[place, :], rs.at[land]).start)
-                pl.when(core == 1)(to_next.start)
-            else:
-                send(lambda m=m: box.at[m], lambda place=place: c.at[place, :],
-                     ("offer", m, t), device, land)
+        to = (me.ctx + o) % 32
+        place = rows_at((to % 2) * CAND + TOK + m * BLOCK, BLOCK, 64)
+        send(lambda m=m: box.at[m], lambda place=place: c.at[place, :], ("offer", m), (me.dp, to))
     shared = [(lambda k: own, lambda k: c.at[crows_of(k, TOK), :]),
               (lambda k: bias2.at[crows_of(1 - k, CAND), :], lambda k: bias2.at[crows_of(k, CAND), :])]
     for i, (src, dst) in enumerate(pairs + shared):
         send(lambda src=src: src(1 - core), lambda dst=dst: dst(core), ("sib", i), sib)
+
+    def offered_rows(k):
+        return c.at[rows_at(k * CAND + TOK, 4 * BLOCK, TOK), :]
 
     my_rows = rows_at(me.z * 32, 32, 32)
     zrows = lambda o: rows_at(z_at[o % 8] * 32, 32, 32)
@@ -289,6 +280,9 @@
             send(ref, ref, ("ring", n, way), at_z(1 if way == 0 else 7))
 
     along_z(1, 1)
+    for m in range(4):
+        got_it(c.at[rows_at(core * CAND + TOK + m * BLOCK, BLOCK, 64), :], ("offer", m))
+    send(lambda: offered_rows(core), lambda: offered_rows(core), "offer_on", sib)
 
     def weight_part(rows, side, step, name):
         got_it(w.at[rows, cols_of(0, side, step)], name)
@@ -375,22 +369,34 @@
         for i in range(2):
             got_it(y1r.at[f * 2 + i], ("ry1", f * 2 + i))
         acc[slot] = acc[slot] + (y1r[f * 2].astype(f32) + y1r[f * 2 + 1].astype(f32))
+        if f == 1:
+            low[...] = acc[slot].astype(bf)
+            for o in range(1, 16):
+                send(lambda o=o: low.at[rows_at(chip_at[o] * 16, 16, 16), :], lambda o=o: low_in.at[o],
+                     ("rz", f, o), me.in_ctx(chip_at[o], core))
+            return
         for o in range(1, 8):
-            send(lambda o=o: acc.at[slot, zrows(o), :], lambda o=o: zbuf.at[f * 8 + o],
-                 ("rz", f, o), at_z(o))
+            send(lambda o=o: acc.at[slot, zrows(o), :], lambda o=o: zbuf.at[o], ("rz", f, o), at_z(o))
 
     def add_side(f):
+        if f == 1:
+            total = acc[SLOT[f, 0, 0], rows_at(chip * 16, 16, 16), :]
+            for o in range(1, 16):
+                got_it(low_in.at[o], ("rz", f, o))
+                total = total + low_in[o].astype(f32)
+            fin[f] = total
+            return
         total = acc[SLOT[f, 0, 0], my_rows, :]
         for o in range(1, 8):
-            got_it(zbuf.at[f * 8 + o], ("rz", f, o))
-            total = total + zbuf[f * 8 + o]
-        part[f] = total
-        send(lambda: part.at[f, rows_at((1 - me.xl) * 16, 16, 16), :], lambda: side_in.at[f],
-             ("pair", f), me.side())
+            got_it(zbuf.at[o], ("rz", f, o))
+            total = total + zbuf[o]
+        part[...] = total
+        send(lambda: part.at[rows_at((1 - me.xl) * 16, 16, 16), :], lambda: side_in, "pair", me.side())
 
     def finish(f):
-        got_it(side_in.at[f], ("pair", f))
-        fin[f] = part[f, rows_at(me.xl * 16, 16, 16), :] + side_in[f]
+        if f == 0:
+            got_it(side_in, "pair")
+            fin[f] = part[rows_at(me.xl * 16, 16, 16), :] + side_in[...]
         for o in range(8):
             for k in range(2):
                 if o == 0 and k == 0:
@@ -422,9 +428,7 @@
         cp.wait()
     for i, (_, dst) in enumerate(pairs + shared):
         got_it(dst(1 - core), ("sib", i))
-    for m in range(4):
-        for g in range(2):
-            got_it(c.at[pl.ds(g * CAND + TOK + m * BLOCK, BLOCK), :], land0 + m * 2 + g)
+    got_it(offered_rows(1 - core), "offer_on")
     zero = jnp.zeros((2 * CAND, ROPE), bf)
     rp = c[:, LAT:]
     rope_a[...] = jnp.concatenate([rp, zero], axis=1)
@@ -498,51 +502,36 @@
 
     last = after.index(("add_z", 1)) + 1
     act(after[:last])
+    late = [op for op in after[last:] if op[1] == 1]
     ra = rope_acc[...]
-    full = jnp.concatenate([lat[...], ra[:, :ROPE] + ra[:, ROPE:]], axis=1)
-    cg[...] = full
-    cgl[...] = full.astype(bf)
-
-    back0 = sem("back_in", 8)
+    cg[...] = jnp.concatenate([lat[...], ra[:, :ROPE] + ra[:, ROPE:]], axis=1)
+    send(lambda: cg.at[crows_of(1 - core, CAND), :], lambda: own2, "back_o", sib)
+    act(op for op in after[last:] if op[1] == 0)
+
+    got_it(own2, "back_o")
+    mine = cg[crows_of(core, CAND), :] + own2[...]
     for m, o in enumerate(offsets):
-        for g in range(2):
-            target = (chip * 2 + g + 32 - o) % 32
-            src = lambda m=m, g=g: cgl.at[pl.ds(g * CAND + TOK + m * BLOCK, BLOCK), :]
-            dst = lambda m=m: got.at[m * 2 + core]
-            land = back0 + m * 2 + core
-            if m == 0 and g == 1:
-                at = sem("to_last")
-                to_last = rdma(src(), dst(), ss.at[at], rs.at[land], (me.dp, target))
-                pl.when(core == 0)(pltpu.make_async_copy(src(), dst(), rs.at[land]).start)
-                pl.when(core == 1)(to_last.start)
-            else:
-                send(src, dst, ("back", m, g), (me.dp, target), land)
+        cgl[m] = mine[TOK + m * BLOCK:TOK + (m + 1) * BLOCK].astype(bf)
+        send(lambda m=m: cgl.at[m], lambda m=m: got.at[m], ("back", m), (me.dp, (me.ctx + 32 - o) % 32))
 
     ncol = lambda k: out_n.at[:, col(k, 4096)]
     rcol_ = lambda k: out_r.at[:, col(k, 2048)]
-    send(lambda: cg.at[crows_of(1 - core, TOK), :], lambda: own2, "back_o", sib)
     send(lambda: gqn.at[rows_of(1 - core), :], lambda: ncol(core), "back_n", sib)
     send(lambda: gqr.at[rows_of(1 - core), :], lambda: rcol_(core), "back_r", sib)
     first_late = len(local)
     copy(gqn.at[qrow, :], ncol(core))
     copy(gqr.at[qrow, :], rcol_(core))
 
-    act(after[last:-2])
-
-    got_it(own2, "back_o")
-    total = cg[crow, :] + own2[...]
-    first, second = total[:BLOCK], total[BLOCK:]
+    act(late)
+
+    first, second = mine[:BLOCK], mine[BLOCK:TOK]
     for m in range(4):
-        for k in range(2):
-            got_it(got.at[m * 2 + k], back0 + m * 2 + k)
-        rows = got[m * 2].astype(f32) + got[m * 2 + 1].astype(f32)
+        got_it(got.at[m], ("back", m))
+        rows = got[m].astype(f32)
         nil = jnp.zeros_like(rows)
         first = first + jnp.where(offer[m] == 0, rows, nil)
         second = second + jnp.where(offer[m] == 0, nil, rows)
-    out_l[0:BLOCK, :] = first
-    out_l[BLOCK:TOK, :] = second
-
-    act(after[-2:])
+    out_l[...] = jnp.concatenate([first, second], axis=0).T
     for f in range(2):
         copy(fin.at[f, rows_at(core * 8, 8), :], out_cols(f, core, me.dp))
     got_it(ncol(1 - core), "back_n")
@@ -556,8 +545,6 @@
                 got_it(out_cols(f, who, (me.dp + 8 - o) % 8), ("w", f, o, k))
     for cp in local[first_late:]:
         cp.wait()
-    pl.when(core == 1)(to_next.wait_send)
-    pl.when(core == 1)(to_last.wait_send)
     for src, at in sends:
         rdma(src(), src(), ss.at[at], rs.at[at], sib).wait_send()
     assert sem.count <= NSEM, sem.count
@@ -573,7 +560,7 @@
         out_shape=(
             jax.ShapeDtypeStruct((TOK, HEADS * NOPE), bf),
             jax.ShapeDtypeStruct((TOK, HEADS * ROPE), bf),
-            jax.ShapeDtypeStruct((TOK, LAT + ROPE), f32),
+            jax.ShapeDtypeStruct((LAT + ROPE, TOK), f32),
             jax.ShapeDtypeStruct((8, 2 * HALF), f32),
         ),
         in_specs=[smem, smem] + [ANY] * 4 + [VMEM, VMEM],
@@ -584,8 +571,8 @@
             v((2, HALF_HEADS, TOK), f32), v((2 * CAND, LAT + ROPE), bf), v((2 * CAND, TOK), bf),
             v((LAT, HALF), bf), v((3, 8, WIDE), bf), v((3, 8, LONG), bf), v((32, LONG), f32),
             v((2 * TOK, 4096), bf), v((2 * TOK, 2048), bf),
-            v((2 * CAND, LAT + ROPE), f32), v((2 * CAND, LAT + ROPE), bf),
-            v((8, BLOCK, LAT + ROPE), bf), v((TOK, LAT + ROPE), f32),
+            v((2 * CAND, LAT + ROPE), f32), v((4, BLOCK, LAT + ROPE), bf),
+            v((4, BLOCK, LAT + ROPE), bf), v((CAND, LAT + ROPE), f32),
             v((2 * CAND, 128), bf), v((2 * CAND, 128), bf), v((LAT, 2 * CAND), bf),
             v((2 * CAND, LAT), f32), v((2 * CAND, 128), f32),
             v((16, LAT, WIDE), f32),
@@ -593,8 +580,8 @@
             v((8, 128, WIDE), bf),
             v((4, 128, WIDE), bf), v((4, 128, WIDE), bf),
             v((4, 256, WIDE), bf), v((4, 256, WIDE), bf),
-            v((16, 32, WIDE), f32), v((2, 32, WIDE), f32), v((2, 16, WIDE), f32),
-            v((2, 16, WIDE), f32),
+            v((8, 32, WIDE), f32), v((32, WIDE), f32), v((16, WIDE), f32),
+            v((LAT, WIDE), bf), v((16, 16, WIDE), bf), v((2, 16, WIDE), f32),
             dma((NSEM,)), dma((NSEM,)), dma((16,)),
         ],
         compiler_params=pltpu.CompilerParams(
@@ -603,11 +590,37 @@
     )(selected, offered, qn, qr, go, lt, own_t, upw)
 
 
+def hand_over_kernel(a, b, c, d, out_a, out_b, out_c, out_d):
+    out_a[...] = a[...]
+    out_b[...] = b[...]
+    out_c[...] = c[...]
+    out_d[...] = d[...]
+
+
+def hand_over(*arrays):
+    steps = 8
+    specs = []
+    for a in arrays:
+        if a.shape[0] == 8:
+            specs.append(pl.BlockSpec((8, a.shape[1] // steps), lambda i: (0, i)))
+        else:
+            specs.append(pl.BlockSpec((a.shape[0] // steps, a.shape[1]), lambda i: (i, 0)))
+    return pl.pallas_call(
+        hand_over_kernel,
+        grid=(steps,),
+        out_shape=tuple(jax.ShapeDtypeStruct(a.shape, a.dtype) for a in arrays),
+        in_specs=specs,
+        out_specs=tuple(specs),
+        compiler_params=pltpu.CompilerParams(vmem_limit_bytes=60 << 20),
+        name="hand_over",
+    )(*arrays)
+
+
 def shards(q_nope, q_rope, grad_out, log_total, kv_latent, up_weight, selected, offered):
-    out_n, out_r, out_l, out_w = fused_call(
-        selected[0], offered[0], q_nope[0], q_rope[0], grad_out[0], log_total[0], kv_latent[0].T,
-        up_weight)
-    return (out_n[None], out_r[None], out_l[None], out_w)
+    out_n, out_r, out_l, out_w = hand_over(*fused_call(
+        selected[0], offered[0].T, q_nope[0], q_rope[0], grad_out[0], log_total[0], kv_latent[0].T,
+        up_weight))
+    return (out_n[None], out_r[None], out_l.T[None], out_w)
 
 
 def solution(mesh):

time: 130 us -> 113 us (0.87)
  Pallas kernels: 121 us -> 112 us
  local copies, waits for them, and re-layouts: 8.06 us -> 0 us
    pallas_call x1, Pallas kernels: 121 us -> 106 us  [fused_call(): pl.pallas_call(fused_kernel, out_shape=(jax.ShapeDtypeStruct((TOK, HEADS...]
    unnamed x8 -> x0, local copies, waits for them, and re-layouts: 6.69 us -> none
    pallas_call x0 -> x1, Pallas kernels: none -> 6.41 us  [hand_over(): pl.pallas_call(hand_over_kernel, grid=(steps,), out_shape=tuple((jax.Shap...]
    squeeze x1 -> x0, local copies, waits for them, and re-layouts: 1.37 us -> none  [shards(): offered[0]]
where the time goes in v4:
time: 113 us
  Pallas kernels  112 us (99%)
    pallas_call x1, Pallas kernels, fused_call(): pl.pallas_call(fused_kernel, out_shape=(jax.ShapeDtypeStruct((TOK, HEADS...  106 us
    pallas_call x1, Pallas kernels, hand_over(): pl.pallas_call(hand_over_kernel, grid=(steps,), out_shape=tuple((jax.Shap...  6.41 us

profile of v4, /device:TPU:1, one launch (start us, length us, event | category | flops | bytes accessed | tf_op | source)
XLA Modules:
  0.0 112.7 jit_solution(2963101143954236170)
XLA Ops:
  0.6 105.6 %fused_backward.1 = (bf16[128,8192]{1,0:T(8,128)(2,1)}, bf16[128,4096]{1,0:T(8,128)(2,1)}, f32[320,128]{1,0:T(8,128)}, f32[8,16384]{1,0:T(8,128)}) custom-call(s32[2,3]{1,0:T(2,128)} %bitcast.22, s32[4,32]{1,0:T(4,128)} %bitcast.21, bf16[128,8192]{1,0:T(8,128)(2,1)} %bitcast.16, bf16[128,4096]{1,0:T(8,128)(2,1)} %bitcast.18, bf16[128,8192]{1,0:T(8,128)(2,1)} %bitcast.17, ...), custom_call_target="tpu_custom_call" | custom-call | tf_op jit(solution)/shard_map/fused_backward/pallas_call | solution.py:558
  106.2 6.4 %hand_over.1 = (bf16[128,8192]{1,0:T(8,128)(2,1)}, bf16[128,4096]{1,0:T(8,128)(2,1)}, f32[320,128]{1,0:T(8,128)}, f32[8,16384]{1,0:T(8,128)}) custom-call(bf16[128,8192]{1,0:T(8,128)(2,1)} %get-tuple-element.12.a, bf16[128,4096]{1,0:T(8,128)(2,1)} %get-tuple-element.13.b, f32[320,128]{1,0:T(8,128)} %get-tuple-element.14.c, f32[8,16384]{1,0:T(8,128)} %get-tuple-element.15.d), custom_call_target="tpu_custom_call" | custom-call | tf_op jit(solution)/shard_map/hand_over/pallas_call | solution.py:608

commit v5 on v4

--- a/solution.py
+++ b/solution.py
@@ -22,7 +22,6 @@
 offsets = (1, 2, 3, 4)
 MESH = pl.DeviceIdType.MESH
 NT = (((1,), (1,)), ((), ()))
-TN = (((0,), (0,)), ((), ()))
 VMEM = pl.BlockSpec(memory_space=pltpu.VMEM)
 ANY = pl.BlockSpec(memory_space=pl.ANY)
 
@@ -83,18 +82,18 @@
 
 
 PLAN = (
-    ("cross", 0, 0), ("along_y", 0), ("relay", 0, 0), ("unit", 0, 0, 0), ("cross", 0, 1),
-    ("cross", 0, 3), ("down", 0), ("up", 0), ("along_z", 1, 2), ("unit", 0, 0, 1),
-    ("unit", 0, 0, 3), ("cross", 0, 2), ("relay", 0, 1), ("unit", 0, 1, 0), ("relay", 0, 3),
-    ("along_z", 1, 3), ("unit", 0, 0, 2), ("relay", 0, 2), ("unit", 0, 1, 1), ("add_x", 0, 1),
-    ("unit", 0, 1, 3), ("along_z", 1, 4), ("unit", 0, 1, 2), ("add_x", 0, 2), ("add_x", 0, 3),
-    ("add_cross", 0, 1), ("add_x", 0, 0), ("unit", 1, 1, 2), ("add_x", 1, 2), ("add_cross", 0, 2),
-    ("unit", 1, 1, 1), ("unit", 1, 1, 0), ("add_y2", 0), ("add_cross", 0, 3), ("add_cross", 0, 0),
-    ("unit", 1, 1, 3), ("add_x", 1, 1), ("add_x", 1, 3), ("add_x", 1, 0), ("add_cross", 1, 2),
-    ("add_y1", 0, 0), ("add_y1", 0, 1), ("unit", 1, 0, 2), ("add_cross", 1, 1), ("unit", 1, 0, 1),
-    ("add_cross", 1, 3), ("add_y2", 1), ("unit", 1, 0, 3), ("add_z", 0), ("add_cross", 1, 0),
-    ("add_y1", 1, 0), ("add_y1", 1, 1), ("unit", 1, 0, 0), ("add_z", 1), ("add_side", 0),
-    ("finish", 0), ("add_side", 1), ("finish", 1),
+    ("along_y", 0), ("unit", 0, 0, 0), ("cross", 0, 0), ("cross", 0, 3), ("up", 0),
+    ("cross", 0, 1), ("relay", 0, 0), ("down", 0), ("unit", 0, 0, 3), ("along_z", 1, 2),
+    ("relay", 0, 3), ("cross", 0, 2), ("unit", 0, 0, 2), ("relay", 0, 1), ("unit", 0, 1, 0),
+    ("along_z", 1, 3), ("relay", 0, 2), ("unit", 0, 1, 3), ("add_x", 0, 3), ("unit", 0, 1, 1),
+    ("unit", 0, 1, 2), ("add_x", 0, 2), ("along_z", 1, 4), ("add_x", 0, 1), ("add_cross", 0, 3),
+    ("add_x", 0, 0), ("unit", 0, 0, 1), ("add_cross", 0, 2), ("unit", 1, 1, 2), ("unit", 1, 1, 3),
+    ("add_x", 1, 2), ("add_cross", 0, 1), ("add_x", 1, 3), ("add_y2", 0), ("unit", 1, 1, 1),
+    ("add_cross", 0, 0), ("unit", 1, 1, 0), ("add_x", 1, 1), ("add_cross", 1, 2),
+    ("add_y1", 0, 0), ("add_y1", 0, 1), ("unit", 1, 0, 3), ("add_cross", 1, 3), ("unit", 1, 0, 2),
+    ("add_x", 1, 0), ("add_cross", 1, 1), ("add_y2", 1), ("unit", 1, 0, 1), ("add_z", 0),
+    ("add_cross", 1, 0), ("add_y1", 1, 0), ("add_y1", 1, 1), ("unit", 1, 0, 0), ("add_z", 1),
+    ("add_side", 0), ("finish", 0), ("add_side", 1), ("finish", 1),
 )
 UNITS = [op[1:] for op in PLAN if op[0] == "unit"]
 SLOT = {u: i for i, u in enumerate(UNITS)}
@@ -451,54 +450,60 @@
         xh = me.xh + side - 2 * me.xh * side
         p = half * 8 + xh * 4 + (me.y + step) % 4
 
-        rcol = pl.ds(pl.multiple_of(p * 128, 128), 128)
-        whs, kvs = [], []
-        for e in range(2):
-            wh = w[:, pl.ds(pl.multiple_of(p * 512 + e * 256, 256), 256)]
-            whs.append(wh)
-            kvs.append(mm(c[:, :LAT], wh).astype(bf))
+        rcol = col(p, 128)
+        pair = col(p, 512)
+        hcol = [col(p * 2 + e, 128) for e in range(2)]
+        keys = [slice(g * CAND, (g + 1) * CAND) for g in range(2)]
+        qs = [slice(g * TOK, (g + 1) * TOK) for g in range(2)]
+        expanded = mm(c[:, :LAT], w[:, pair]).astype(bf)
+        kvs = [expanded[:, :256], expanded[:, 256:]]
+
+        def kcat(g, e):
+            rope = rope_a if e == 0 else rope_b
+            return jnp.concatenate([kvs[e][keys[g], :128], rope[keys[g], :]], axis=1)
+
+        def qcat(g, e):
+            return jnp.concatenate([qn2[qs[g], hcol[e]], qr2[qs[g], rcol]], axis=1)
+
+        both = []
+        for g in range(2):
+            gos = [go2[qs[g], hcol[e]] for e in range(2)]
+            both.append(jnp.concatenate(
+                [jnp.concatenate([gos[0], z128], axis=1),
+                 jnp.concatenate([z128, gos[1]], axis=1)], axis=0))
+        sg, low_p = {}, {}
+        for g in range(2):
+            vals = jnp.concatenate([kvs[0][keys[g], 128:], kvs[1][keys[g], 128:]], axis=1)
+            dp_t = dg(vals, both[g], NT)
+            scores = [dg(kcat(g, e), qcat(g, e), NT) for e in range(2)]
+            for e in range(2):
+                shift = bias2[keys[g], :].astype(f32) - lt2[g, pl.ds(p * 2 + e, 1), :]
+                p_t = jnp.exp(scores[e] * SCALE + shift)
+                d = dp_t[:, e * 128:(e + 1) * 128]
+                rd = jnp.sum(p_t * d, axis=0, keepdims=True)
+                sg[g, e] = (p_t * (d - rd)).astype(bf)
+                low_p[g, e] = p_t.astype(bf)
         kgs = [[None, None], [None, None]]
         for g in range(2):
-            rows = slice(g * CAND, (g + 1) * CAND)
-            qs = slice(g * TOK, (g + 1) * TOK)
-            qrp = qr2[qs, rcol]
-            hcol = [pl.ds(pl.multiple_of(p * 256 + e * 128, 128), 128) for e in range(2)]
-            gos = [go2[qs, hcol[e]] for e in range(2)]
-            bd = jnp.concatenate(
-                [jnp.concatenate([gos[0], z128], axis=1),
-                 jnp.concatenate([z128, gos[1]], axis=1)], axis=0)
-            vals = jnp.concatenate([kvs[0][rows, 128:], kvs[1][rows, 128:]], axis=1)
-            dp_t = dg(vals, bd, NT)
-            gr, rk, lows = None, [], []
+            vg = mm(jnp.concatenate([low_p[g, 0], low_p[g, 1]], axis=1), both[g]).astype(bf)
+            rk = []
             for e in range(2):
-                rope = (rope_a if e == 0 else rope_b)[rows, :]
-                kcat = jnp.concatenate([kvs[e][rows, :128], rope], axis=1)
-                qcat = jnp.concatenate([qn2[qs, hcol[e]], qrp], axis=1)
-                s_t = dg(kcat, qcat, NT)
-                shift = bias2[rows, :].astype(f32) - lt2[g, pl.ds(p * 2 + e, 1), :]
-                p_t = jnp.exp(s_t * SCALE + shift)
-                d = dp_t[:, e * 128:(e + 1) * 128]
-                rd = jnp.sum(p_t * d, axis=0, keepdims=True)
-                sg = (p_t * (d - rd)).astype(bf)
-                lows.append(p_t.astype(bf))
-                gq = dg(sg, kcat, TN) * SCALE
-                gqn[qs, hcol[e]] = gq[:, :128].astype(bf)
+                kg = mm(sg[g, e], qcat(g, e)) * SCALE
+                rk.append(kg[:, 128:])
+                kgs[e][g] = jnp.concatenate(
+                    [kg[:, :128].astype(bf), vg[:, e * 128:(e + 1) * 128]], axis=1)
+            rope_acc[keys[g], :] += jnp.where(lane < ROPE, rk[0], rk[1])
+            turned = jnp.concatenate([sg[g, 0], sg[g, 1]], axis=1).T
+            gr = None
+            for e in range(2):
+                gq = mm(turned[e * 128:(e + 1) * 128], kcat(g, e)) * SCALE
+                gqn[qs[g], hcol[e]] = gq[:, :128].astype(bf)
                 gr = gq[:, 128:] if gr is None else gr + gq[:, 128:]
-                kg = mm(sg, qcat) * SCALE
-                rk.append(kg[:, 128:])
-                kgs[e][g] = kg[:, :128].astype(bf)
-            gqr[qs, rcol] = gr.astype(bf)
-            vg = mm(jnp.concatenate(lows, axis=1), bd).astype(bf)
-            for e in range(2):
-                kgs[e][g] = jnp.concatenate([kgs[e][g], vg[:, e * 128:(e + 1) * 128]], axis=1)
-            rope_acc[rows, :] += jnp.where(lane < ROPE, rk[0], rk[1])
-        tot = None
-        for e in range(2):
-            kga = jnp.concatenate(kgs[e], axis=0)
-            acc[s, :, e * 256:(e + 1) * 256] = mm(ct[...], kga)
-            t = dg(kga, whs[e], NT)
-            tot = t if tot is None else tot + t
-        lat[...] += tot
+            gqr[qs[g], rcol] = gr.astype(bf)
+        kga = jnp.concatenate([jnp.concatenate(kgs[e], axis=0) for e in range(2)], axis=1)
+        acc[s] = mm(ct[...], kga)
+        for g in range(2):
+            lat[keys[g], :] += dg(kga[keys[g]], w[:, pair], NT)
 
     last = after.index(("add_z", 1)) + 1
     act(after[:last])
@@ -590,27 +595,37 @@
     )(selected, offered, qn, qr, go, lt, own_t, upw)
 
 
-def hand_over_kernel(a, b, c, d, out_a, out_b, out_c, out_d):
-    out_a[...] = a[...]
-    out_b[...] = b[...]
-    out_c[...] = c[...]
-    out_d[...] = d[...]
+def hand_over_kernel(*refs):
+    count = (len(refs) - 2) // 3
+    sources, results, held = refs[:count], refs[count:2 * count], refs[2 * count:3 * count]
+    sem_in, sem_out = refs[3 * count:]
+    parts = []
+    for src, dst, buf in zip(sources, results, held):
+        pieces = src.shape[0] // 32 if src.shape[0] == TOK else 1
+        size = src.shape[0] // pieces
+        for i in range(pieces):
+            rows = pl.ds(i * size, size)
+            at = len(parts)
+            parts.append((
+                pltpu.make_async_copy(src.at[rows, :], buf.at[rows, :], sem_in.at[at]),
+                pltpu.make_async_copy(buf.at[rows, :], dst.at[rows, :], sem_out.at[at])))
+    for into, _ in parts:
+        into.start()
+    for into, out in parts:
+        into.wait()
+        out.start()
+    for _, out in parts:
+        out.wait()
 
 
 def hand_over(*arrays):
-    steps = 8
-    specs = []
-    for a in arrays:
-        if a.shape[0] == 8:
-            specs.append(pl.BlockSpec((8, a.shape[1] // steps), lambda i: (0, i)))
-        else:
-            specs.append(pl.BlockSpec((a.shape[0] // steps, a.shape[1]), lambda i: (i, 0)))
+    dma = pltpu.SemaphoreType.DMA
     return pl.pallas_call(
         hand_over_kernel,
-        grid=(steps,),
         out_shape=tuple(jax.ShapeDtypeStruct(a.shape, a.dtype) for a in arrays),
-        in_specs=specs,
-        out_specs=tuple(specs),
+        in_specs=[ANY] * len(arrays),
+        out_specs=(ANY,) * len(arrays),
+        scratch_shapes=[pltpu.VMEM(a.shape, a.dtype) for a in arrays] + [dma((16,)), dma((16,))],
         compiler_params=pltpu.CompilerParams(vmem_limit_bytes=60 << 20),
         name="hand_over",
     )(*arrays)

time: 113 us -> 107 us (0.947)
  Pallas kernels: 112 us -> 105 us
    pallas_call x1, Pallas kernels: 106 us -> 102 us  [fused_call(): pl.pallas_call(fused_kernel, out_shape=(jax.ShapeDtypeStruct((TOK, HEADS...]
    pallas_call x1, Pallas kernels: 6.41 us -> 3.35 us  [hand_over(): pl.pallas_call(hand_over_kernel, out_shape=tuple((jax.ShapeDtypeStruct(a....]
where the time goes in v5:
time: 107 us; the launch traced here: 106 us
  Pallas kernels  105 us (98%)
    pallas_call x1, Pallas kernels, fused_call(): pl.pallas_call(fused_kernel, out_shape=(jax.ShapeDtypeStruct((TOK, HEADS...  102 us
    pallas_call x1, Pallas kernels, hand_over(): pl.pallas_call(hand_over_kernel, out_shape=tuple((jax.ShapeDtypeStruct(a....  3.35 us

profile of v5, /device:TPU:1, one launch (start us, length us, event | category | flops | bytes accessed | tf_op | source)
XLA Modules:
  0.0 106.0 jit_solution(7689484957512095540)
XLA Ops:
  0.6 102.0 %fused_backward.1 = (bf16[128,8192]{1,0:T(8,128)(2,1)}, bf16[128,4096]{1,0:T(8,128)(2,1)}, f32[320,128]{1,0:T(8,128)}, f32[8,16384]{1,0:T(8,128)}) custom-call(s32[2,3]{1,0:T(2,128)} %bitcast.22, s32[4,32]{1,0:T(4,128)} %bitcast.21, bf16[128,8192]{1,0:T(8,128)(2,1)} %bitcast.16, bf16[128,4096]{1,0:T(8,128)(2,1)} %bitcast.18, bf16[128,8192]{1,0:T(8,128)(2,1)} %bitcast.17, ...), custom_call_target="tpu_custom_call" | custom-call | tf_op jit(solution)/shard_map/fused_backward/pallas_call | solution.py:563
  102.7 3.4 %hand_over.1 = (bf16[128,8192]{1,0:T(8,128)(2,1)}, bf16[128,4096]{1,0:T(8,128)(2,1)}, f32[320,128]{1,0:T(8,128)}, f32[8,16384]{1,0:T(8,128)}) custom-call(bf16[128,8192]{1,0:T(8,128)(2,1)} %get-tuple-element.12.refs_0_, bf16[128,4096]{1,0:T(8,128)(2,1)} %get-tuple-element.13.refs_1_, f32[320,128]{1,0:T(8,128)} %get-tuple-element.14.refs_2_, ...), custom_call_target="tpu_custom_call" | custom-call | tf_op jit(solution)/shard_map/hand_over/pallas_call | solution.py:623

commit v6 on v5

--- a/solution.py
+++ b/solution.py
@@ -82,18 +82,20 @@
 
 
 PLAN = (
-    ("along_y", 0), ("unit", 0, 0, 0), ("cross", 0, 0), ("cross", 0, 3), ("up", 0),
-    ("cross", 0, 1), ("relay", 0, 0), ("down", 0), ("unit", 0, 0, 3), ("along_z", 1, 2),
-    ("relay", 0, 3), ("cross", 0, 2), ("unit", 0, 0, 2), ("relay", 0, 1), ("unit", 0, 1, 0),
-    ("along_z", 1, 3), ("relay", 0, 2), ("unit", 0, 1, 3), ("add_x", 0, 3), ("unit", 0, 1, 1),
-    ("unit", 0, 1, 2), ("add_x", 0, 2), ("along_z", 1, 4), ("add_x", 0, 1), ("add_cross", 0, 3),
-    ("add_x", 0, 0), ("unit", 0, 0, 1), ("add_cross", 0, 2), ("unit", 1, 1, 2), ("unit", 1, 1, 3),
-    ("add_x", 1, 2), ("add_cross", 0, 1), ("add_x", 1, 3), ("add_y2", 0), ("unit", 1, 1, 1),
-    ("add_cross", 0, 0), ("unit", 1, 1, 0), ("add_x", 1, 1), ("add_cross", 1, 2),
-    ("add_y1", 0, 0), ("add_y1", 0, 1), ("unit", 1, 0, 3), ("add_cross", 1, 3), ("unit", 1, 0, 2),
-    ("add_x", 1, 0), ("add_cross", 1, 1), ("add_y2", 1), ("unit", 1, 0, 1), ("add_z", 0),
-    ("add_cross", 1, 0), ("add_y1", 1, 0), ("add_y1", 1, 1), ("unit", 1, 0, 0), ("add_z", 1),
-    ("add_side", 0), ("finish", 0), ("add_side", 1), ("finish", 1),
+    ("along_y", 0), ("cross", 0, 0), ("along_z", 1, 1), ("unit", 0, 0, 0), ("cross", 0, 3),
+    ("down", 0), ("cross", 0, 1), ("relay", 0, 0), ("up", 0), ("along_z", 1, 2),
+    ("unit", 0, 0, 3), ("relay", 0, 3), ("cross", 0, 2), ("relay", 0, 1), ("unit", 0, 1, 0),
+    ("along_z", 1, 3), ("relay", 0, 2), ("unit", 0, 1, 3), ("add_x", 0, 3), ("unit", 0, 0, 1),
+    ("unit", 0, 1, 2), ("add_x", 0, 2), ("along_z", 1, 4), ("unit", 0, 1, 1), ("add_x", 0, 1),
+    ("add_x", 0, 0), ("add_cross", 0, 3), ("unit", 0, 0, 2), ("add_cross", 0, 2),
+    ("unit", 1, 1, 1), ("unit", 1, 1, 2), ("add_cross", 0, 1), ("add_x", 1, 2), ("unit", 1, 0, 1),
+    ("add_cross", 0, 0), ("add_x", 1, 1), ("add_y2", 0), ("unit", 1, 1, 3), ("add_y1_far", 0, 0),
+    ("add_y1_far", 0, 1), ("add_cross", 1, 2), ("add_x", 1, 3), ("unit", 1, 0, 2),
+    ("add_cross", 1, 1), ("add_y1", 0, 1), ("add_y1", 0, 0), ("unit", 1, 1, 0), ("add_x", 1, 0),
+    ("add_cross", 1, 3), ("unit", 1, 0, 3), ("add_y2", 1), ("add_y1_far", 1, 0), ("add_z", 0),
+    ("add_y1_far", 1, 1), ("add_y1", 1, 0), ("add_cross", 1, 0), ("add_y1", 1, 1),
+    ("unit", 1, 0, 0), ("add_z", 1), ("add_side", 0), ("finish", 0), ("add_side", 1),
+    ("finish", 1),
 )
 UNITS = [op[1:] for op in PLAN if op[0] == "unit"]
 SLOT = {u: i for i, u in enumerate(UNITS)}
@@ -113,7 +115,8 @@
         return self.at[name]
 
 
-NSEM = 256
+ARRIVALS = 132
+SENDS = 48
 
 
 def fused_kernel(
@@ -143,15 +146,19 @@
     seen = set()
 
     def send(src, dst, name, device):
-        at = sem(name)
-        rdma(src(), dst(), ss.at[at], rs.at[at], device).start()
+        if len(sends) < SENDS:
+            at = len(sends)
+        else:
+            old, at = sends.pop(0)
+            rdma(old(), old(), ss.at[at], rs.at[0], sib).wait_send()
+        rdma(src(), dst(), ss.at[at], rs.at[sem(name)], device).start()
         sends.append((src, at))
 
     def got_it(ref, name):
         if name not in seen:
             seen.add(name)
             at = sem(name)
-            rdma(ref, ref, ss.at[at], rs.at[at], sib).wait_recv()
+            rdma(ref, ref, ss.at[0], rs.at[at], sib).wait_recv()
 
     def copy(src, dst):
         cp = pltpu.make_async_copy(src, dst, ls.at[len(local)])
@@ -272,13 +279,14 @@
         return w.at[rows, full_long if n < 4 else quarters[way]]
 
     def along_z(f, n):
+        if n == 1:
+            need_block(0, 0, 0)
         for way in range(2):
             if n > 1:
                 got_it(ring_in(n - 1, way), ("ring", n - 1, way))
             ref = lambda way=way: ring_ref(n, way)
             send(ref, ref, ("ring", n, way), at_z(1 if way == 0 else 7))
 
-    along_z(1, 1)
     for m in range(4):
         got_it(c.at[rows_at(core * CAND + TOK + m * BLOCK, BLOCK, 64), :], ("offer", m))
     send(lambda: offered_rows(core), lambda: offered_rows(core), "offer_on", sib)
@@ -351,23 +359,31 @@
             y2s[at] = acc[SLOT[f, 0, 2], i * 128:(i + 1) * 128, :].astype(bf)
             send(lambda at=at: y2s.at[at], lambda at=at: y2r.at[at], ("ry2", at), me.ring(step))
 
+    def add_y1_far(f, i):
+        step = (1, 3)[i]
+        crossed(f, step)
+        at = f * 4 + i * 2
+        far = slice((1 - i) * 128, (2 - i) * 128)
+        y1s[at] = acc[SLOT[f, 0, step], far, :].astype(bf)
+        send(lambda: y1s.at[at], lambda: y1r.at[at], ("ry1", at), me.ring(step))
+
     def add_y1(f, i):
         step = (1, 3)[i]
-        crossed(f, step)
-        at = f * 2 + i
-        got_it(y2r.at[at], ("ry2", at))
-        slot = SLOT[f, 0, step]
-        near_half, far = slice(i * 128, (i + 1) * 128), slice((1 - i) * 128, (2 - i) * 128)
-        y1s[at, near_half, :] = (acc[slot, near_half, :] + y2r[at].astype(f32)).astype(bf)
-        y1s[at, far, :] = acc[slot, far, :].astype(bf)
+        got_it(y2r.at[f * 2 + i], ("ry2", f * 2 + i))
+        at = f * 4 + i * 2 + 1
+        near_half = slice(i * 128, (i + 1) * 128)
+        y1s[at] = (acc[SLOT[f, 0, step], near_half, :] + y2r[f * 2 + i].astype(f32)).astype(bf)
         send(lambda: y1s.at[at], lambda: y1r.at[at], ("ry1", at), me.ring(step))
 
     def add_z(f):
         slot = SLOT[f, 0, 0]
         crossed(f, 0)
+        for at in range(f * 4, f * 4 + 4):
+            got_it(y1r.at[at], ("ry1", at))
         for i in range(2):
-            got_it(y1r.at[f * 2 + i], ("ry1", f * 2 + i))
-        acc[slot] = acc[slot] + (y1r[f * 2].astype(f32) + y1r[f * 2 + 1].astype(f32))
+            rows = slice(i * 128, (i + 1) * 128)
+            near_in, far_in = f * 4 + i * 2 + 1, f * 4 + (1 - i) * 2
+            acc[slot, rows, :] += y1r[near_in].astype(f32) + y1r[far_in].astype(f32)
         if f == 1:
             low[...] = acc[slot].astype(bf)
             for o in range(1, 16):
@@ -409,7 +425,8 @@
 
     actions = dict(
         along_y=along_y, along_z=along_z, cross=cross, up=up, down=down, relay=relay, add_x=add_x,
-        add_cross=add_cross, add_y2=add_y2, add_y1=add_y1, add_z=add_z, add_side=add_side,
+        add_cross=add_cross, add_y2=add_y2, add_y1=add_y1,
+        add_y1_far=add_y1_far, add_z=add_z, add_side=add_side,
         finish=finish, unit=need_block)
     before, events = [], []
     for op in PLAN:
@@ -515,9 +532,8 @@
 
     got_it(own2, "back_o")
     mine = cg[crows_of(core, CAND), :] + own2[...]
-    for m, o in enumerate(offsets):
+    for m in range(4):
         cgl[m] = mine[TOK + m * BLOCK:TOK + (m + 1) * BLOCK].astype(bf)
-        send(lambda m=m: cgl.at[m], lambda m=m: got.at[m], ("back", m), (me.dp, (me.ctx + 32 - o) % 32))
 
     ncol = lambda k: out_n.at[:, col(k, 4096)]
     rcol_ = lambda k: out_r.at[:, col(k, 2048)]
@@ -528,6 +544,8 @@
     copy(gqr.at[qrow, :], rcol_(core))
 
     act(late)
+    for m, o in enumerate(offsets):
+        send(lambda m=m: cgl.at[m], lambda m=m: got.at[m], ("back", m), (me.dp, (me.ctx + 32 - o) % 32))
 
     first, second = mine[:BLOCK], mine[BLOCK:TOK]
     for m in range(4):
@@ -551,8 +569,8 @@
     for cp in local[first_late:]:
         cp.wait()
     for src, at in sends:
-        rdma(src(), src(), ss.at[at], rs.at[at], sib).wait_send()
-    assert sem.count <= NSEM, sem.count
+        rdma(src(), src(), ss.at[at], rs.at[0], sib).wait_send()
+    assert sem.count == ARRIVALS, sem.count
 
 
 def fused_call(selected, offered, qn, qr, go, lt, own_t, upw):
@@ -584,10 +602,10 @@
             v((8, 128, WIDE), bf), v((8, 128, WIDE), bf), v((8, 128, WIDE), bf),
             v((8, 128, WIDE), bf),
             v((4, 128, WIDE), bf), v((4, 128, WIDE), bf),
-            v((4, 256, WIDE), bf), v((4, 256, WIDE), bf),
+            v((8, 128, WIDE), bf), v((8, 128, WIDE), bf),
             v((8, 32, WIDE), f32), v((32, WIDE), f32), v((16, WIDE), f32),
             v((LAT, WIDE), bf), v((16, 16, WIDE), bf), v((2, 16, WIDE), f32),
-            dma((NSEM,)), dma((NSEM,)), dma((16,)),
+            dma((SENDS,)), dma((ARRIVALS,)), dma((8,)),
         ],
         compiler_params=pltpu.CompilerParams(
             collective_id=0, has_side_effects=True, vmem_limit_bytes=56 << 20),
@@ -625,7 +643,7 @@
         out_shape=tuple(jax.ShapeDtypeStruct(a.shape, a.dtype) for a in arrays),
         in_specs=[ANY] * len(arrays),
         out_specs=(ANY,) * len(arrays),
-        scratch_shapes=[pltpu.VMEM(a.shape, a.dtype) for a in arrays] + [dma((16,)), dma((16,))],
+        scratch_shapes=[pltpu.VMEM(a.shape, a.dtype) for a in arrays] + [dma((10,)), dma((10,))],
         compiler_params=pltpu.CompilerParams(vmem_limit_bytes=60 << 20),
         name="hand_over",
     )(*arrays)

time: 107 us -> 103 us (0.963)
  Pallas kernels: 105 us -> 102 us
    pallas_call x1, Pallas kernels: 102 us -> 99 us  [fused_call(): pl.pallas_call(fused_kernel, out_shape=(jax.ShapeDtypeStruct((TOK, HEADS...]
where the time goes in v6:
time: 103 us
  Pallas kernels  102 us (99%)
    pallas_call x1, Pallas kernels, fused_call(): pl.pallas_call(fused_kernel, out_shape=(jax.ShapeDtypeStruct((TOK, HEADS...  99 us
    pallas_call x1, Pallas kernels, hand_over(): pl.pallas_call(hand_over_kernel, out_shape=tuple((jax.ShapeDtypeStruct(a....  3.25 us

profile of v6, /device:TPU:1, one launch (start us, length us, event | category | flops | bytes accessed | tf_op | source)
XLA Modules:
  0.0 102.9 jit_solution(12917773007487936563)
XLA Ops:
  0.6 99.0 %fused_backward.1 = (bf16[128,8192]{1,0:T(8,128)(2,1)}, bf16[128,4096]{1,0:T(8,128)(2,1)}, f32[320,128]{1,0:T(8,128)}, f32[8,16384]{1,0:T(8,128)}) custom-call(s32[2,3]{1,0:T(2,128)} %bitcast.22, s32[4,32]{1,0:T(4,128)} %bitcast.21, bf16[128,8192]{1,0:T(8,128)(2,1)} %bitcast.16, bf16[128,4096]{1,0:T(8,128)(2,1)} %bitcast.18, bf16[128,8192]{1,0:T(8,128)(2,1)} %bitcast.17, ...), custom_call_target="tpu_custom_call" | custom-call | tf_op jit(solution)/shard_map/fused_backward/pallas_call | solution.py:581
  99.7 3.2 %hand_over.1 = (bf16[128,8192]{1,0:T(8,128)(2,1)}, bf16[128,4096]{1,0:T(8,128)(2,1)}, f32[320,128]{1,0:T(8,128)}, f32[8,16384]{1,0:T(8,128)}) custom-call(bf16[128,8192]{1,0:T(8,128)(2,1)} %get-tuple-element.12.refs_0_, bf16[128,4096]{1,0:T(8,128)(2,1)} %get-tuple-element.13.refs_1_, f32[320,128]{1,0:T(8,128)} %get-tuple-element.14.refs_2_, ...), custom_call_target="tpu_custom_call" | custom-call | tf_op jit(solution)/shard_map/hand_over/pallas_call | solution.py:641

commit v7 on v6

--- a/solution.py
+++ b/solution.py
@@ -82,20 +82,20 @@
 
 
 PLAN = (
-    ("along_y", 0), ("cross", 0, 0), ("along_z", 1, 1), ("unit", 0, 0, 0), ("cross", 0, 3),
-    ("down", 0), ("cross", 0, 1), ("relay", 0, 0), ("up", 0), ("along_z", 1, 2),
-    ("unit", 0, 0, 3), ("relay", 0, 3), ("cross", 0, 2), ("relay", 0, 1), ("unit", 0, 1, 0),
-    ("along_z", 1, 3), ("relay", 0, 2), ("unit", 0, 1, 3), ("add_x", 0, 3), ("unit", 0, 0, 1),
-    ("unit", 0, 1, 2), ("add_x", 0, 2), ("along_z", 1, 4), ("unit", 0, 1, 1), ("add_x", 0, 1),
-    ("add_x", 0, 0), ("add_cross", 0, 3), ("unit", 0, 0, 2), ("add_cross", 0, 2),
-    ("unit", 1, 1, 1), ("unit", 1, 1, 2), ("add_cross", 0, 1), ("add_x", 1, 2), ("unit", 1, 0, 1),
-    ("add_cross", 0, 0), ("add_x", 1, 1), ("add_y2", 0), ("unit", 1, 1, 3), ("add_y1_far", 0, 0),
-    ("add_y1_far", 0, 1), ("add_cross", 1, 2), ("add_x", 1, 3), ("unit", 1, 0, 2),
-    ("add_cross", 1, 1), ("add_y1", 0, 1), ("add_y1", 0, 0), ("unit", 1, 1, 0), ("add_x", 1, 0),
-    ("add_cross", 1, 3), ("unit", 1, 0, 3), ("add_y2", 1), ("add_y1_far", 1, 0), ("add_z", 0),
-    ("add_y1_far", 1, 1), ("add_y1", 1, 0), ("add_cross", 1, 0), ("add_y1", 1, 1),
-    ("unit", 1, 0, 0), ("add_z", 1), ("add_side", 0), ("finish", 0), ("add_side", 1),
-    ("finish", 1),
+    ("along_y", 0), ("along_z", 1, 1), ("cross", 0, 0), ("unit", 0, 0, 0), ("down", 0),
+    ("cross", 0, 3), ("up", 0), ("along_z", 1, 2), ("cross", 0, 1), ("relay", 0, 0),
+    ("unit", 0, 0, 3), ("relay", 0, 3), ("cross", 0, 2), ("unit", 0, 0, 2), ("relay", 0, 1),
+    ("along_z", 1, 3), ("unit", 0, 0, 1), ("relay", 0, 2), ("unit", 0, 1, 3), ("unit", 0, 1, 1),
+    ("add_x", 0, 3), ("along_z", 1, 4), ("unit", 0, 1, 2), ("add_x", 0, 2), ("unit", 0, 1, 0),
+    ("add_cross", 0, 3), ("add_x", 0, 1), ("add_x", 0, 0), ("unit", 1, 1, 2), ("add_x", 1, 2),
+    ("add_cross", 0, 2), ("unit", 1, 1, 1), ("add_cross", 0, 1), ("add_x", 1, 1),
+    ("unit", 1, 0, 2), ("add_y2", 0), ("add_cross", 0, 0), ("add_y1_far", 0, 1),
+    ("unit", 1, 1, 3), ("add_x", 1, 3), ("add_cross", 1, 2), ("add_y1_far", 0, 0),
+    ("unit", 1, 1, 0), ("add_y1", 0, 0), ("add_cross", 1, 1), ("add_y1", 0, 1), ("unit", 1, 0, 1),
+    ("add_cross", 1, 3), ("add_x", 1, 0), ("unit", 1, 0, 3), ("add_y2", 1), ("add_z", 0),
+    ("add_y1_far", 1, 0), ("add_y1_far", 1, 1), ("unit", 1, 0, 0), ("add_cross", 1, 0),
+    ("add_y1", 1, 0), ("add_y1", 1, 1), ("add_z", 1), ("add_side", 0), ("finish", 0),
+    ("add_side", 1), ("finish", 1),
 )
 UNITS = [op[1:] for op in PLAN if op[0] == "unit"]
 SLOT = {u: i for i, u in enumerate(UNITS)}

time: 103 us -> 101 us (0.981)
    pallas_call x1, Pallas kernels: 99 us -> 97.5 us  [fused_call(): pl.pallas_call(fused_kernel, out_shape=(jax.ShapeDtypeStruct((TOK, HEADS...]
where the time goes in v7:
time: 101 us
  Pallas kernels  101 us (100%)
    pallas_call x1, Pallas kernels, fused_call(): pl.pallas_call(fused_kernel, out_shape=(jax.ShapeDtypeStruct((TOK, HEADS...  97.5 us
    pallas_call x1, Pallas kernels, hand_over(): pl.pallas_call(hand_over_kernel, out_shape=tuple((jax.ShapeDtypeStruct(a....  3.25 us

profile of v7, /device:TPU:1, one launch (start us, length us, event | category | flops | bytes accessed | tf_op | source)
XLA Modules:
  0.0 101.4 jit_solution(13344087883861170385)
XLA Ops:
  0.6 97.5 %fused_backward.1 = (bf16[128,8192]{1,0:T(8,128)(2,1)}, bf16[128,4096]{1,0:T(8,128)(2,1)}, f32[320,128]{1,0:T(8,128)}, f32[8,16384]{1,0:T(8,128)}) custom-call(s32[2,3]{1,0:T(2,128)} %bitcast.22, s32[4,32]{1,0:T(4,128)} %bitcast.21, bf16[128,8192]{1,0:T(8,128)(2,1)} %bitcast.16, bf16[128,4096]{1,0:T(8,128)(2,1)} %bitcast.18, bf16[128,8192]{1,0:T(8,128)(2,1)} %bitcast.17, ...), custom_call_target="tpu_custom_call" | custom-call | tf_op jit(solution)/shard_map/fused_backward/pallas_call | solution.py:581
  98.1 3.2 %hand_over.1 = (bf16[128,8192]{1,0:T(8,128)(2,1)}, bf16[128,4096]{1,0:T(8,128)(2,1)}, f32[320,128]{1,0:T(8,128)}, f32[8,16384]{1,0:T(8,128)}) custom-call(bf16[128,8192]{1,0:T(8,128)(2,1)} %get-tuple-element.12.refs_0_, bf16[128,4096]{1,0:T(8,128)(2,1)} %get-tuple-element.13.refs_1_, f32[320,128]{1,0:T(8,128)} %get-tuple-element.14.refs_2_, ...), custom_call_target="tpu_custom_call" | custom-call | tf_op jit(solution)/shard_map/hand_over/pallas_call | solution.py:641
